TPU v7x, 256 devices: a whole 4x4x8 slice. The times are simulated.
256 devices in a mesh: ctx: 16 (over z, core), head: 16 (over y, x).
Axes of the slice: x: 4, y: 4, z: 8, core: 2. Of those that a mesh axis runs over, the one named last changes fastest.
Arguments:
- stretch_keys: bfloat16 [16, 65536, 128], P('head', 'ctx'), may hold values from -6 to 6
- stretch_values: bfloat16 [16, 65536, 128], P('head', 'ctx'), may hold values from -6 to 6
- stretch_assign: int32 [16, 65536], P('head', 'ctx'), may hold values from 0 to 4095, as said below
- centroid_keys: float32 [16, 4096, 128], P('head'), may hold values from -3.5 to 3.5
- centroid_values: float32 [16, 4096, 128], P('head'), may hold values from -3 to 3
- cluster_counts: float32 [16, 4096], P('head'), may hold values from 64 to 1024
- cache_keys: bfloat16 [16, 131072, 128], P('head', 'ctx'), may hold values from -6 to 6
- cache_values: bfloat16 [16, 131072, 128], P('head', 'ctx'), may hold values from -6 to 6
- block_cluster: int32 [16, 8192], P('head', 'ctx'), may hold values from 0 to 4095
- selected: int32 [4, 16, 64], P(None, 'head'), may hold values from 0 to 4095
- queries: bfloat16 [4, 64, 16, 128], P(None, 'head'), may hold values from -90 to 90
Outputs:
- new_keys: float32 [16, 4096, 128], P('head', 'ctx')
- new_values: float32 [16, 4096, 128], P('head', 'ctx')
- new_counts: float32 [16, 4096], P('head', 'ctx')
- attended: bfloat16 [4, 16, 64, 128], P(None, 'head', 'ctx')
Inputs may be any that keep to these rules, and one draw needn't show every extreme that they name: `stretch_assign`: within each aligned block of 4096 prefill positions of one head, the clusters of one group j // (4096 / 16) are named at most 320 times; in every block some group is named exactly 320 times.
All inputs are finite; a program needn't handle non-finite values.
Results may differ from a plain program's by a relative error of at most 0.0045.
Values may be sent and summed in bfloat16 or wider, within the bound.
A program may use at most 128 MiB of HBM per device.

v0:
```python
import jax
import jax.numpy as jnp
from jax import lax
from jax.sharding import PartitionSpec as P


def in_one_piece(arrays, axis, split_dim, concat_dim, along):
    columns = [a.reshape(*a.shape[:along], -1) for a in arrays]
    both = jnp.concatenate(columns, axis=along)
    whole, at, outs = (
        lax.all_to_all(both, axis, split_axis=split_dim, concat_axis=concat_dim, tiled=True),
        0,
        [],
    )
    for a, column in zip(arrays, columns):
        slab = whole[..., at : at + column.shape[along]]
        outs.append(slab.reshape(*slab.shape[:along], *a.shape[along:]))
        at += column.shape[along]
    return tuple(outs)


def member_of(ids, chosen):
    return jnp.any(ids[..., :, None] == chosen[..., None, :], axis=-1)


def shards(
    stretch_keys,
    stretch_values,
    stretch_assign,
    centroid_keys,
    centroid_values,
    cluster_counts,
    cache_keys,
    cache_values,
    block_cluster,
    selected,
    queries,
):
    clusters = centroid_keys.shape[1]
    width = centroid_keys.shape[2]
    local_heads = centroid_keys.shape[0]
    groups = lax.axis_size("ctx")
    owned = clusters // groups
    first = lax.axis_index("ctx") * owned
    positions = stretch_keys.shape[1]
    joined = jnp.concatenate([stretch_keys, stretch_values], axis=2)
    capacity = positions // groups + positions // (4 * groups)
    owner = stretch_assign // owned
    owner_onehot = (owner[..., None] == jnp.arange(groups, dtype=jnp.int32)).astype(jnp.int32)
    ranking = jnp.sum((jnp.cumsum(owner_onehot, axis=1) - 1) * owner_onehot, axis=-1)
    target = owner * capacity + ranking
    inside = stretch_assign - owner * owned

    def place_rows(rows, labels_in, where):
        buffer = jnp.zeros((groups * capacity, rows.shape[-1]), rows.dtype).at[where].set(rows)
        marks = jnp.full((groups * capacity,), -1, jnp.int32).at[where].set(labels_in)
        return (buffer, marks)

    buffer, marks = jax.vmap(place_rows)(joined, inside, target)
    buffer = buffer.reshape(local_heads, groups, capacity, 2 * width)
    marks = marks.reshape(local_heads, groups, capacity)
    arrived, arrived_marks = (
        lax.all_to_all(buffer, "ctx", split_axis=1, concat_axis=1, tiled=True),
        lax.all_to_all(marks, "ctx", split_axis=1, concat_axis=1, tiled=True),
    )
    arrived = arrived.reshape(local_heads, groups * capacity, 2 * width)
    arrived_marks = arrived_marks.reshape(local_heads, groups * capacity)
    owner_hits = arrived_marks[..., None] == jnp.arange(owned, dtype=jnp.int32)
    sums = jnp.einsum(
        "htc,htd->hcd", owner_hits.astype(jnp.bfloat16), arrived, preferred_element_type=jnp.float32
    )
    counts = jnp.sum(owner_hits, axis=1).astype(jnp.float32)
    old_keys = lax.dynamic_slice_in_dim(centroid_keys, first, owned, 1)
    old_values = lax.dynamic_slice_in_dim(centroid_values, first, owned, 1)
    old_counts = lax.dynamic_slice_in_dim(cluster_counts, first, owned, 1)
    total = old_counts + counts
    new_keys = (old_counts[..., None] * old_keys + sums[..., :width]) / total[..., None]
    new_values = (old_counts[..., None] * old_values + sums[..., width:]) / total[..., None]
    rows_q = lax.all_to_all(queries, "head", split_axis=2, concat_axis=1, tiled=True)
    steps = rows_q.shape[0]
    query_rows = rows_q.shape[1]
    scale = width ** (-0.5)
    hp = lax.Precision.HIGHEST
    block_hit = member_of(
        jnp.broadcast_to(block_cluster[None], (steps,) + block_cluster.shape), selected
    )
    block_len = cache_keys.shape[1] // block_cluster.shape[1]
    cache_hit = jnp.broadcast_to(block_hit[..., None], block_hit.shape + (block_len,)).reshape(
        steps, local_heads, cache_keys.shape[1]
    )
    stretch_hit = member_of(
        jnp.broadcast_to(stretch_assign[None], (steps,) + stretch_assign.shape), selected
    )
    own_ids = first + jnp.arange(owned, dtype=jnp.int32)
    centre_free = jnp.logical_not(
        member_of(jnp.broadcast_to(own_ids, (steps, local_heads, owned)), selected)
    )
    s_cache = (
        jnp.einsum("sqhd,htd->shqt", rows_q, cache_keys, preferred_element_type=jnp.float32) * scale
    )
    s_stretch = (
        jnp.einsum("sqhd,htd->shqt", rows_q, stretch_keys, preferred_element_type=jnp.float32)
        * scale
    )
    s_centre = (
        jnp.einsum("sqhd,hcd->shqc", rows_q.astype(jnp.float32), new_keys, precision=hp) * scale
    )
    s_centre = s_centre + jnp.log(total)[None, :, None, :]
    s_cache = jnp.where(cache_hit[:, :, None, :], s_cache, -1e30)
    s_stretch = jnp.where(stretch_hit[:, :, None, :], s_stretch, -1e30)
    s_centre = jnp.where(centre_free[:, :, None, :], s_centre, -1e30)
    peak = jnp.maximum(
        jnp.maximum(jnp.max(s_cache, -1), jnp.max(s_stretch, -1)), jnp.max(s_centre, -1)
    )
    p_cache = jnp.where(cache_hit[:, :, None, :], jnp.exp(s_cache - peak[..., None]), 0.0)
    p_stretch = jnp.where(stretch_hit[:, :, None, :], jnp.exp(s_stretch - peak[..., None]), 0.0)
    p_centre = jnp.where(centre_free[:, :, None, :], jnp.exp(s_centre - peak[..., None]), 0.0)
    whole = jnp.sum(p_cache, -1) + jnp.sum(p_stretch, -1) + jnp.sum(p_centre, -1)
    acc = jnp.einsum(
        "shqt,htd->shqd",
        p_cache.astype(jnp.bfloat16),
        cache_values,
        preferred_element_type=jnp.float32,
    )
    acc = acc + jnp.einsum(
        "shqt,htd->shqd",
        p_stretch.astype(jnp.bfloat16),
        stretch_values,
        preferred_element_type=jnp.float32,
    )
    acc = acc + jnp.einsum("shqc,hcd->shqd", p_centre, new_values, precision=hp)
    share = query_rows // groups
    peaks, totals, parts = in_one_piece((peak, whole, acc), "ctx", 2, 0, 3)
    peaks = peaks.reshape(groups, steps, local_heads, share)
    totals = totals.reshape(groups, steps, local_heads, share)
    parts = parts.reshape(groups, steps, local_heads, share, width)
    top = jnp.max(peaks, axis=0)
    factor = jnp.exp(peaks - top[None])
    summed = jnp.sum(totals * factor, axis=0)
    gathered = jnp.sum(parts * factor[..., None], axis=0)
    result = gathered / summed[..., None]
    return (new_keys, new_values, total, result.astype(jnp.bfloat16))


def solution(mesh):
    in_specs = (
        P("head", "ctx", None),
        P("head", "ctx", None),
        P("head", "ctx"),
        P("head", None, None),
        P("head", None, None),
        P("head", None),
        P("head", "ctx", None),
        P("head", "ctx", None),
        P("head", "ctx"),
        P(None, "head", None),
        P(None, "head", None, None),
    )
    out_specs = (
        P("head", "ctx", None),
        P("head", "ctx", None),
        P("head", "ctx"),
        P(None, "head", "ctx", None),
    )
    return jax.shard_map(shards, mesh=mesh, in_specs=in_specs, out_specs=out_specs, check_vma=False)
```

profile of v0, /device:TPU:1, one launch (start us, length us, event | category | flops | bytes accessed | tf_op | source)
XLA Modules:
  0.0 180.9 jit_solution(2655864518918970642)
XLA Ops:
  0.7 1.0 multiply_subtract_fusion
  1.6 0.7 copy.46
  2.4 8.3 %reduce-window.6 = s32[1,16,32,128]{3,2,1,0:T(8,128)S(1)} reduce-window(s32[1,16,32,128]{3,2,1,0:T(8,128)} %bitcast.145, s32[]{:T(128)} %constant.17.clone.1), window={size=1x1x1x128 pad=0_0x0_0x0_0x127_0}, to_apply=%region_0.1 | reduce-window | flops 8323072 | bytes 524292 | tf_op jit(solution)/shard_map/reduce-window
  10.7 0.7 reshape.498
  12.1 0.8 broadcast.253
  12.9 1.0 reshape.501
  13.9 1.0 fusion.51
  15.0 0.8 and_reduce_fusion
  15.8 0.8 fusion.60
  16.6 15.5 %scatter_custom_fusion = s32[5120]{0:T(1024)S(1)} fusion(s32[4096]{0:T(1024)S(1)} %broadcast_select_fusion, s32[4096]{0:T(1024)S(1)} %bitcast.161, s32[]{:T(128)} %constant.22.clone.1), kind=kCustom, calls=%fused_computation.83 | custom fusion | bytes 20484
  32.1 0.7 reshape.502
  32.8 10.0 %all-to-all-start = ((s32[1,16,320]{2,0,1:T(1,128)}), s32[1,16,320]{2,0,1:T(1,128)S(1)}, u32[]{:S(2)}, u32[]{:S(2)}) async-start(s32[1,16,320]{2,0,1:T(1,128)} %reshape.502), calls=%async_computation | async-start | bytes 49152 | tf_op jit(solution)/shard_map/all_to_all | solution.py:64
  42.8 1.5 copy.35
  44.3 5.9 %all-to-all-done = s32[1,16,320]{2,0,1:T(1,128)S(1)} async-done(((s32[1,16,320]{2,0,1:T(1,128)}), s32[1,16,320]{2,0,1:T(1,128)S(1)}, u32[]{:S(2)}, u32[]{:S(2)}) %all-to-all-start) | async-done | bytes 20512 | tf_op jit(solution)/shard_map/all_to_all | solution.py:64
  50.2 6.8 %all-to-all-start.2 = ((bf16[4,4,16,128]{3,1,0,2:T(4,128)(2,1)}), bf16[4,4,16,128]{3,1,0,2:T(4,128)(2,1)S(1)}, u32[]{:S(2)}, u32[]{:S(2)}) async-start(bf16[4,4,16,128]{3,1,0,2:T(4,128)(2,1)} %copy.35), calls=%async_computation.2 | async-start | bytes 131072 | tf_op jit(solution)/shard_map/all_to_all | solution.py:79
  57.0 20.0 %scatter_custom_fusion.1 = bf16[5120,256]{1,0:T(8,128)(2,1)} fusion(s32[4096]{0:T(1024)S(1)} %broadcast_select_fusion, bf16[1,4096,128]{2,1,0:T(8,128)(2,1)} %param.12, bf16[]{:T(256)} %constant.82, bf16[1,4096,128]{2,1,0:T(8,128)(2,1)S(1)} %copy-done.3, bf16[]{:T(256)} %constant.46.clone.1), kind=kCustom, calls=%fused_computation.29 | custom fusion | flops 4194304 | bytes 4718596
  77.0 4.9 %all-to-all-start.1 = ((bf16[1,16,320,256]{3,2,0,1:T(8,128)(2,1)}), bf16[1,16,320,256]{3,2,0,1:T(8,128)(2,1)}, u32[]{:S(2)}, u32[]{:S(2)}) async-start(bf16[1,16,320,256]{3,2,0,1:T(8,128)(2,1)} %bitcast.142), calls=%async_computation.1 | async-start | bytes 5242880 | tf_op jit(solution)/shard_map/all_to_all | solution.py:63
  83.1 1.2 broadcast_in_dim.99
  84.2 0.7 compare_reduce_fusion
  85.1 2.3 %convert_reduce_fusion = s32[256]{0:T(256)S(1)} fusion(s32[5120]{0:T(1024)S(1)} %eq.124), kind=kLoop, calls=%fused_computation.10 | loop fusion | flops 3931904 | bytes 21504 | tf_op jit(solution)/shard_map/reduce_sum | solution.py:72
  87.4 1.3 fusion.68
  88.7 2.7 %fusion.72 = (f32[4,64]{1,0:T(4,128)S(1)}, f32[4,1,64,4096]{3,2,0,1:T(8,128)}) fusion(bf16[4,64,128]{2,1,0:T(8,128)(2,1)S(1)} %bitcast.147, bf16[1,4096,128]{2,1,0:T(8,128)(2,1)S(1)} %copy-done.3, pred[4,4096]{1,0:T(4,128)(4,1)S(1)} %compare_reduce_fusion), kind=kOutput, calls=%fused_computation.100 | convolution fusion | flops 271580928 | bytes 5325824 | tf_op jit(solution)/shard_map/sqhd,htd->shqt/dot_general | solution.py:102
  91.4 4.6 %fusion.71 = (f32[4,64]{1,0:T(4,128)S(1)}, f32[4,1,64,8192]{3,2,0,1:T(8,128)}) fusion(bf16[4,64,128]{2,1,0:T(8,128)(2,1)S(1)} %bitcast.148, bf16[1,8192,128]{2,1,0:T(8,128)(2,1)S(1)} %copy-done, pred[4,8192]{1,0:T(4,128)(4,1)S(1)} %copy-done.7), kind=kOutput, calls=%fused_computation.99 | convolution fusion | flops 543162112 | bytes 10585088 | tf_op jit(solution)/shard_map/sqhd,htd->shqt/dot_general | solution.py:99
  96.1 45.7 %all-to-all-done.1 = bf16[1,16,320,256]{3,2,0,1:T(8,128)(2,1)} async-done(((bf16[1,16,320,256]{3,2,0,1:T(8,128)(2,1)}), bf16[1,16,320,256]{3,2,0,1:T(8,128)(2,1)}, u32[]{:S(2)}, u32[]{:S(2)}) %all-to-all-start.1) | async-done | bytes 2621472 | tf_op jit(solution)/shard_map/all_to_all | solution.py:63
  141.8 5.6 %fusion.31 = f32[1,256,256]{2,1,0:T(8,128)S(1)} fusion(bf16[5120,256]{1,0:T(8,128)(2,1)} %bitcast.11, s32[5120]{0:T(1024)S(1)} %copy-done.10), kind=kOutput, calls=%fused_computation.40 | convolution fusion | flops 672399360 | bytes 2904064 | tf_op jit(solution)/shard_map/htc,htd->hcd/dot_general | solution.py:69
  147.4 1.8 fusion.53
  149.9 1.5 fusion.19
  151.4 1.0 fusion.16
  153.3 2.0 %fusion.3 = f32[4,64]{1,0:T(4,128)S(1)} fusion(f32[4,1,64,8192]{3,2,0,1:T(8,128)S(1)} %copy-done.2, f32[4,64]{1,0:T(4,128)S(1)} %maximum_maximum_fusion, pred[4,8192]{1,0:T(4,128)(4,1)S(1)} %copy-done.8), kind=kLoop, calls=%fused_computation.7 | loop fusion | flops 6291200 | bytes 8423424 | tf_op jit(solution)/shard_map/reduce_sum | solution.py:118
  155.6 5.5 %fusion.43 = f32[128,4,64]{0,2,1:T(8,128)S(1)} fusion(f32[4,64,128]{2,1,0:T(8,128)S(1)} %copy-done.18, bf16[1,8192,128]{2,1,0:T(8,128)(2,1)} %param.18, f32[4,1,64,8192]{3,2,0,1:T(8,128)} %get-tuple-element.16, f32[4,64]{1,0:T(4,128)S(1)} %maximum_maximum_fusion, pred[4,8192]{1,0:T(4,128)(4,1)S(1)} %copy-done.8), kind=kOutput, calls=%fused_computation.47 | convolution fusion | flops 543195136 | bytes 10781696 | tf_op jit(solution)/shard_map/shqt,htd->shqd/dot_general | solution.py:119
  161.9 16.9 %all_to_all.43 = f32[4,1,64,130]{3,0,1,2:T(4,128)S(1)} all-to-all(f32[4,1,64,130]{3,0,1,2:T(4,128)S(1)} %copy.39), channel_id=1, replica_groups=mesh['ctx'=16,'head'=16] {'ctx'}, dimensions={2} | all-to-all | bytes 266240 | tf_op jit(solution)/shard_map/all_to_all | solution.py:11
  180.2 0.7 fusion.64
  (77 shorter events, 6.0 us)
Async XLA Ops:
  0.6 90.8 %copy-start = (bf16[1,8192,128]{2,1,0:T(8,128)(2,1)S(1)}, bf16[1,8192,128]{2,1,0:T(8,128)(2,1)}, u32[]{:S(2)}) copy-start(bf16[1,8192,128]{2,1,0:T(8,128)(2,1)} %param.17) | copy-start | bytes 6291460
  0.6 56.3 %copy-start.3 = (bf16[1,4096,128]{2,1,0:T(8,128)(2,1)S(1)}, bf16[1,4096,128]{2,1,0:T(8,128)(2,1)}, u32[]{:S(2)}) copy-start(bf16[1,4096,128]{2,1,0:T(8,128)(2,1)} %param.11) | copy-start | bytes 3145732
  32.8 17.3 %all-to-all-start = ((s32[1,16,320]{2,0,1:T(1,128)}), s32[1,16,320]{2,0,1:T(1,128)S(1)}, u32[]{:S(2)}, u32[]{:S(2)}) async-start(s32[1,16,320]{2,0,1:T(1,128)} %reshape.502), calls=%async_computation | async-start | bytes 49152 | tf_op jit(solution)/shard_map/all_to_all | solution.py:64
  50.2 26.8 %all-to-all-start.2 = ((bf16[4,4,16,128]{3,1,0,2:T(4,128)(2,1)}), bf16[4,4,16,128]{3,1,0,2:T(4,128)(2,1)S(1)}, u32[]{:S(2)}, u32[]{:S(2)}) async-start(bf16[4,4,16,128]{3,1,0,2:T(4,128)(2,1)} %copy.35), calls=%async_computation.2 | async-start | bytes 131072 | tf_op jit(solution)/shard_map/all_to_all | solution.py:79
  56.9 24.9 %copy-start.12 = (s32[4,1,64]{2,1,0:T(1,128)S(1)}, s32[4,1,64]{2,1,0:T(1,128)}, u32[]{:S(2)}) copy-start(s32[4,1,64]{2,1,0:T(1,128)} %param.20) | copy-start | bytes 3076
  56.9 25.6 %copy-start.17 = (s32[1,512]{1,0:T(1,128)S(1)}, s32[1,512]{1,0:T(1,128)}, u32[]{:S(2)}) copy-start(s32[1,512]{1,0:T(1,128)} %param.19) | copy-start | bytes 6148
  57.0 27.3 %copy-start.11 = (s32[1,4096]{1,0:T(1,128)S(1)}, s32[1,4096]{1,0:T(1,128)}, u32[]{:S(2)}) copy-start(s32[1,4096]{1,0:T(1,128)} %param.13) | copy-start | bytes 49156
  77.0 64.8 %all-to-all-start.1 = ((bf16[1,16,320,256]{3,2,0,1:T(8,128)(2,1)}), bf16[1,16,320,256]{3,2,0,1:T(8,128)(2,1)}, u32[]{:S(2)}, u32[]{:S(2)}) async-start(bf16[1,16,320,256]{3,2,0,1:T(8,128)(2,1)} %bitcast.142), calls=%async_computation.1 | async-start | bytes 5242880 | tf_op jit(solution)/shard_map/all_to_all | solution.py:63
  84.2 7.2 %copy-start.7 = (pred[4,8192]{1,0:T(4,128)(4,1)S(1)}, pred[4,8192]{1,0:T(4,128)(4,1)}, u32[]{:S(2)}) copy-start(pred[4,8192]{1,0:T(4,128)(4,1)} %broadcast_in_dim.99) | copy-start | bytes 98308
  85.1 3.5 %copy-start.9 = (s32[5120]{0:T(1024)}, s32[5120]{0:T(1024)S(1)}, u32[]{:S(2)}) copy-start(s32[5120]{0:T(1024)S(1)} %eq.124) | copy-start | bytes 61444
  91.4 50.3 %copy-start.10 = (s32[5120]{0:T(1024)S(1)}, s32[5120]{0:T(1024)}, u32[]{:S(2)}) copy-start(s32[5120]{0:T(1024)} %copy-done.9) | copy-start | bytes 61444
  96.1 51.4 %copy-start.14 = (f32[1,256]{1,0:T(1,128)S(1)}, f32[1,256]{1,0:T(1,128)}, u32[]{:S(2)}) copy-start(f32[1,256]{1,0:T(1,128)} %get-tuple-element.5) | copy-start | bytes 3076
  96.1 51.4 %copy-start.16 = (f32[1,256]{1,0:T(1,128)S(1)}, f32[1,256]{1,0:T(1,128)}, u32[]{:S(2)}) copy-start(f32[1,256]{1,0:T(1,128)} %get-tuple-element.6) | copy-start | bytes 3076
  96.1 53.2 %copy-start.13 = (pred[4,256]{1,0:T(4,128)(4,1)S(1)}, pred[4,256]{1,0:T(4,128)(4,1)}, u32[]{:S(2)}) copy-start(pred[4,256]{1,0:T(4,128)(4,1)} %not.9) | copy-start | bytes 3076
  96.1 53.2 %copy-start.15 = (f32[1,256]{1,0:T(1,128)S(1)}, f32[1,256]{1,0:T(1,128)}, u32[]{:S(2)}) copy-start(f32[1,256]{1,0:T(1,128)} %get-tuple-element.4) | copy-start | bytes 3076
  96.1 53.8 %copy-start.4 = (bf16[1,4096,128]{2,1,0:T(8,128)(2,1)S(1)}, bf16[1,4096,128]{2,1,0:T(8,128)(2,1)}, u32[]{:S(2)}) copy-start(bf16[1,4096,128]{2,1,0:T(8,128)(2,1)} %param.12) | copy-start | bytes 3145732
  141.8 8.1 %copy-start.1 = (f32[4,1,64,4096]{3,2,0,1:T(8,128)S(1)}, f32[4,1,64,4096]{3,2,0,1:T(8,128)}, u32[]{:S(2)}) copy-start(f32[4,1,64,4096]{3,2,0,1:T(8,128)} %get-tuple-element.18) | copy-start | bytes 12582916
  149.2 0.7 copy-start.6
  149.9 3.4 %copy-start.2 = (f32[4,1,64,8192]{3,2,0,1:T(8,128)S(1)}, f32[4,1,64,8192]{3,2,0,1:T(8,128)}, u32[]{:S(2)}) copy-start(f32[4,1,64,8192]{3,2,0,1:T(8,128)} %get-tuple-element.16) | copy-start | bytes 25165828
  149.9 3.4 %copy-start.8 = (pred[4,8192]{1,0:T(4,128)(4,1)S(1)}, pred[4,8192]{1,0:T(4,128)(4,1)}, u32[]{:S(2)}) copy-start(pred[4,8192]{1,0:T(4,128)(4,1)} %broadcast_in_dim.99) | copy-start | bytes 98308
  153.3 2.3 %copy-start.18 = (f32[4,64,128]{2,1,0:T(8,128)S(1)}, f32[4,64,128]{2,1,0:T(8,128)}, u32[]{:S(2)}) copy-start(f32[4,64,128]{2,1,0:T(8,128)} %fusion.19) | copy-start | bytes 393220
  155.6 5.5 %copy-start.5 = (f32[1,256,128]{2,1,0:T(8,128)S(1)}, f32[1,256,128]{2,1,0:T(8,128)}, u32[]{:S(2)}) copy-start(f32[1,256,128]{2,1,0:T(8,128)} %get-tuple-element.9) | copy-start | bytes 393220
where the time goes:
time: 182 us; the launch traced here: 181 us
  waiting for transfers between devices  51.6 us (28%)
  other arithmetic  43.3 us (24%)
  local copies, waits for them, and re-layouts  25.6 us (14%)
  starting transfers between devices  21.6 us (12%)
  matrix products  20.8 us (11%)
  blocking collectives  16.9 us (9%)
    all_to_all x1, waiting for transfers between devices, shards(): lax.all_to_all(buffer, 'ctx', split_axis=1, concat_axis=1, tiled=True)  45.7 us
    unnamed x5, other arithmetic  21.6 us
    unnamed x41, local copies, waits for them, and re-layouts  18.8 us
    all_to_all x1, blocking collectives, in_one_piece(): lax.all_to_all(both, axis, split_axis=split_dim, concat_axis=concat_dim,...  16.9 us
    all_to_all x1, starting transfers between devices, shards(): lax.all_to_all(marks, 'ctx', split_axis=1, concat_axis=1, tiled=True)  9.98 us
    another operation x2, other arithmetic  8.48 us
    all_to_all x1, starting transfers between devices, shards(): lax.all_to_all(queries, 'head', split_axis=2, concat_axis=1, tiled=True)  6.76 us
    all_to_all x1, waiting for transfers between devices, shards(): lax.all_to_all(marks, 'ctx', split_axis=1, concat_axis=1, tiled=True)  5.87 us
  transfers between devices with their start and end apart: 3, of which 2 were waited for; matrix products, arithmetic and copies ran while one was open for 20% of the time, Pallas kernels for 0%

commit v1 on v0

v1 whole, which is shorter than its diff:
```python
import functools
import math

import jax
import jax.numpy as jnp
from jax import lax
from jax.experimental import pallas as pl
from jax.experimental.pallas import tpu as pltpu
from jax.sharding import PartitionSpec as P

MESH = pl.DeviceIdType.MESH
F32 = jnp.float32
BF16 = jnp.bfloat16
LOG2E = math.log2(math.e)
MASKED = -1e30
FLOOR = -1e29
TILE = 512
SEG = 1024
NT = (((1,), (1,)), ((), ()))


def split2(x):
    high = x.astype(BF16)
    return high, (x - high.astype(F32)).astype(BF16)


def split3(x):
    high = x.astype(BF16)
    rest = x - high.astype(F32)
    mid = rest.astype(BF16)
    return high, mid, (rest - mid.astype(F32)).astype(BF16)


def kernel(
    nctx, nhead, owned, steps, width,
    sel, assign, blocks, old_counts, queries, skeys, svals, ckeys, cvals, cent_k, cent_v,
    out_k, out_v, out_n, out_a,
    kv, cen, hits, bias, scores, mrun, acc, lrun, rel, part, own,
    sib_send, sib_recv, ring_send, ring_recv, qsend, qrecv, csend, crecv, fsend, frecv, lsend, lrecv,
    load_sem, q_ss, q_rs, c_ss, c_rs, s_ss, s_rs, r_ss, r_rs, f_ss, f_rs, l_ss, l_rs,
):
    me = lax.axis_index("ctx")
    head = lax.axis_index("head")
    z, core = me // 2, lax.rem(me, 2)
    nz = nctx // 2
    tokens = skeys.shape[1]
    cached = ckeys.shape[1]
    rows = queries.shape[0]
    share = rows // nctx
    stretch_tiles = tokens // TILE
    tiles = (tokens + cached) // TILE

    loads = [
        pltpu.make_async_copy(skeys.at[0], kv.at[pl.ds(0, tokens), pl.ds(0, width)], load_sem.at[0]),
        pltpu.make_async_copy(svals.at[0], kv.at[pl.ds(0, tokens), pl.ds(width, width)], load_sem.at[1]),
        pltpu.make_async_copy(ckeys.at[0], kv.at[pl.ds(tokens, cached), pl.ds(0, width)], load_sem.at[2]),
        pltpu.make_async_copy(cvals.at[0], kv.at[pl.ds(tokens, cached), pl.ds(width, width)], load_sem.at[3]),
        pltpu.make_async_copy(cent_k.at[0, pl.ds(me * owned, owned), :], cen.at[0], load_sem.at[4]),
        pltpu.make_async_copy(cent_v.at[0, pl.ds(me * owned, owned), :], cen.at[1], load_sem.at[5]),
    ]
    for load in loads:
        load.start()

    barrier = pltpu.get_barrier_semaphore()

    def greet(k, _):
        pl.semaphore_signal(barrier, inc=1, device_id={"ctx": lax.rem(me + k, nctx)}, device_id_type=MESH)
        return 0

    def greet_heads(k, _):
        pl.semaphore_signal(barrier, inc=1, device_id={"head": lax.rem(head + k, nhead)}, device_id_type=MESH)
        return 0

    lax.fori_loop(1, nctx, greet, 0)
    lax.fori_loop(1, nhead, greet_heads, 0)

    ids = assign[...]

    iota = lax.broadcasted_iota(jnp.int32, (owned, width), 0).astype(F32).astype(BF16)
    iota = iota.reshape(owned // 16, 16, width)

    def segment(j, offset):
        zd = lax.rem(z + offset, nz)
        rel[0] = (ids - owned * (2 * zd + 1 - core)).astype(F32)
        rel[1] = (ids - owned * (2 * zd + core)).astype(F32)
        part[...] = jnp.zeros_like(part)

        def step(n, _):
            hot = []
            for side in range(2):
                block = rel[side, pl.ds(pl.multiple_of(n * (SEG // 128), 8), SEG // 128), :]
                pieces = []
                for u in range(SEG // 128):
                    row = jnp.broadcast_to(block[u : u + 1, :], (16, 128)).astype(BF16)
                    equal = iota == row[None]
                    pieces.append(jnp.where(equal, jnp.ones((), BF16), jnp.zeros((), BF16)).reshape(owned, 128))
                hot.append(jnp.concatenate(pieces, axis=1))
            hot = jnp.concatenate(hot, axis=0)
            data = kv[pl.ds(pl.multiple_of(n * SEG, SEG), SEG), :]
            part[...] += jnp.dot(hot, data, preferred_element_type=F32)
            return 0

        lax.fori_loop(0, tokens // SEG, step, 0)
        sib_send[j] = part[0:owned, :].astype(BF16)
        own[j] = part[owned : 2 * owned, :]

    def sibling(j):
        return pltpu.make_async_remote_copy(
            sib_send.at[j], sib_recv.at[j], s_ss.at[j], s_rs.at[j],
            device_id={"ctx": 2 * z + 1 - core}, device_id_type=MESH,
        )

    def hop(direction, step, half):
        at = (direction * 4 + step) * 2 + half
        to = lax.rem(z + (1 if direction == 0 else nz - 1), nz)
        return pltpu.make_async_remote_copy(
            ring_send.at[at], ring_recv.at[at], r_ss.at[at], r_rs.at[at],
            device_id={"ctx": 2 * to + core}, device_id_type=MESH,
        )

    def mixed(j, half, arrivals):
        columns = slice(half * width, (half + 1) * width)
        value = own[j, :, columns] + sib_recv[j, :, columns].astype(F32)
        for direction, step in arrivals:
            hop(direction, step, half).wait_recv()
            value = value + ring_recv[(direction * 4 + step) * 2 + half].astype(F32)
        return value

    hops = []

    def forward(j, direction, step):
        sibling(j).wait_recv()
        first = 0 if direction == 0 else 1
        for half in (first, 1 - first):
            arrivals = []
            if step >= 2 or (step == 1 and half == first):
                arrivals = [(direction, step - 1)]
            ring_send[(direction * 4 + step) * 2 + half] = mixed(j, half, arrivals).astype(BF16)
            copy = hop(direction, step, half)
            copy.start()
            hops.append(copy)

    def start_ring():
        sibling(0).wait_recv()
        for direction in (0, 1):
            ring_send[direction * 8 + direction] = mixed(0, direction, []).astype(BF16)
            copy = hop(direction, 0, direction)
            copy.start()
            hops.append(copy)

    def query_copy(k):
        to = lax.rem(head + k, nhead)
        return pltpu.make_async_remote_copy(
            qsend.at[to], qrecv.at[head], q_ss.at[k], q_rs.at[k], device_id={"head": to}, device_id_type=MESH
        )

    def count_copy(k):
        to = lax.rem(me + k, nctx)
        return pltpu.make_async_remote_copy(
            csend.at[to], crecv.at[me], c_ss.at[k], c_rs.at[k], device_id={"ctx": to}, device_id_type=MESH
        )

    def row_copy(k):
        to = lax.rem(me + k, nctx)
        return pltpu.make_async_remote_copy(
            fsend.at[to], frecv.at[me], f_ss.at[k], f_rs.at[k], device_id={"ctx": to}, device_id_type=MESH
        )

    def lse_copy(k):
        to = lax.rem(me + k, nctx)
        return pltpu.make_async_remote_copy(
            lsend.at[to], lrecv.at[me], l_ss.at[k], l_rs.at[k], device_id={"ctx": to}, device_id_type=MESH
        )

    def each(count, act):
        def step(k, _):
            act(k)
            return 0

        lax.fori_loop(1, count, step, 0)

    r_out = lax.broadcasted_iota(jnp.int32, (rows, rows), 0)
    r_in = lax.broadcasted_iota(jnp.int32, (rows, rows), 1)
    per = rows // nhead
    order = jnp.where(r_in == lax.rem(r_out, per) * nhead + r_out // per, 1.0, 0.0).astype(BF16)
    qsend[...] = jnp.dot(order, queries[...], preferred_element_type=F32).astype(BF16).reshape(nhead, per, width)

    loads[0].wait()
    loads[1].wait()
    segment(0, 4)
    pl.semaphore_wait(barrier, nctx - 1 + nhead - 1)
    sibling(0).start()
    each(nhead, lambda k: query_copy(k).start())
    qrecv[head] = qsend[head]
    segment(1, 3)
    sibling(1).start()
    start_ring()
    segment(2, 5)
    sibling(2).start()

    used = owned // 128
    r = lax.broadcasted_iota(jnp.int32, (nctx * 8, 128), 0)
    pattern = jnp.where(lax.rem(r, 8) < used, (r // 8) * used + lax.rem(r, 8), -1)
    pattern = pattern.astype(F32).astype(BF16).reshape(nctx * 8 // 16, 16, 128)
    lanes = lax.broadcasted_iota(jnp.int32, (128, 128), 0).astype(F32).astype(BF16).reshape(8, 16, 128)
    rel[0] = lax.shift_right_logical(ids, 7).astype(F32)
    rel[1] = (ids & 127).astype(F32)
    part[0 : nctx * 8, 0:128] = jnp.zeros((nctx * 8, 128), F32)

    def count_step(n, _):
        both = []
        for side, table in ((0, pattern), (1, lanes)):
            block = rel[side, pl.ds(pl.multiple_of(n * (SEG // 128), 8), SEG // 128), :]
            pieces = []
            for u in range(SEG // 128):
                row = jnp.broadcast_to(block[u : u + 1, :], (16, 128)).astype(BF16)
                equal = table == row[None]
                pieces.append(jnp.where(equal, jnp.ones((), BF16), jnp.zeros((), BF16)).reshape(-1, 128))
            both.append(jnp.concatenate(pieces, axis=1))
        part[0 : nctx * 8, 0:128] += lax.dot_general(both[0], both[1], NT, preferred_element_type=F32)
        return 0

    lax.fori_loop(0, tokens // SEG, count_step, 0)
    csend[...] = part[0 : nctx * 8, 0:128].reshape(nctx, 8, 128)
    each(nctx, lambda k: count_copy(k).start())
    crecv[me] = csend[me]

    nblk = blocks.shape[1]
    lane = lax.broadcasted_iota(jnp.int32, (16, 128), 1)
    sub = lax.broadcasted_iota(jnp.int32, (16, 128), 0)
    spread = sub * 8 + lane // 16
    expanded = []
    for q in range(nblk // 128):
        source = jnp.broadcast_to(blocks[:, q * 128 : (q + 1) * 128], (16, 128))
        expanded.append(jnp.take_along_axis(source, spread, axis=1, mode="promise_in_bounds"))
    mine = me * owned + lax.broadcasted_iota(jnp.int32, (8, 128), 0) * 128
    mine = mine + lax.broadcasted_iota(jnp.int32, (8, 128), 1)
    dense = jnp.concatenate([ids] + expanded + [mine], axis=0)
    trows, crows = tokens // 128, cached // 128
    for s in range(steps):

        def hit(i, seen):
            return seen | (dense == sel[s, i]).astype(jnp.int32)

        seen = lax.fori_loop(0, sel.shape[1], hit, jnp.zeros(dense.shape, jnp.int32), unroll=8)
        hits[s, 0 : trows + crows, :] = jnp.where(seen[: trows + crows] > 0, 0.0, MASKED)
        hits[s, trows + crows :, :] = jnp.where(seen[trows + crows :] > 0, MASKED, 0.0)

    wide = TILE // 128
    copies = share // steps

    def spread_bias(n, _):
        for u in range(wide):
            per_step = [
                jnp.broadcast_to(hits[s, pl.ds(n * wide + u, 1), :], (copies, 128)) for s in range(steps)
            ]
            bias[n, :, u * 128 : (u + 1) * 128] = jnp.concatenate(per_step, axis=0)
        return 0

    lax.fori_loop(0, tiles, spread_bias, 0)

    forward(1, 0, 1)
    forward(2, 1, 1)

    segment(3, 2)
    sibling(3).start()
    segment(4, 6)
    sibling(4).start()

    each(nhead, lambda k: query_copy(k).wait_recv())
    q = qrecv[...].reshape(rows, width)
    factor = width**-0.5 * LOG2E
    mrun[...] = jnp.full(mrun.shape, FLOOR, F32)

    def score(n, _):
        keys = kv[pl.ds(pl.multiple_of(n * TILE, TILE), TILE), 0:width]
        raw = lax.dot_general(q, keys, NT, preferred_element_type=F32) * factor
        masked = (raw.reshape(nctx, share, TILE) + bias[n][None]).reshape(rows, TILE)
        scores[n] = masked
        top = masked[:, 0:128]
        for u in range(1, wide):
            top = jnp.maximum(top, masked[:, u * 128 : (u + 1) * 128])
        mrun[...] = jnp.maximum(mrun[...], top)
        return 0

    loads[2].wait()
    loads[3].wait()
    lax.fori_loop(0, tiles // 2, score, 0)

    forward(3, 0, 2)
    forward(4, 1, 2)
    segment(5, 1)
    sibling(5).start()
    segment(6, 7)
    sibling(6).start()
    lax.fori_loop(tiles // 2, tiles, score, 0)
    forward(5, 0, 3)
    forward(6, 1, 3)
    segment(7, 0)
    sibling(7).start()

    top_here = jnp.max(mrun[...], axis=1, keepdims=True)
    mrun[...] = jnp.broadcast_to(top_here, mrun.shape)
    lrun[...] = jnp.zeros_like(lrun)
    acc[...] = jnp.zeros_like(acc)

    def weigh(n, _):
        top = mrun[...]
        pieces, total = [], lrun[...]
        for u in range(wide):
            p = jnp.exp2(scores[n, :, u * 128 : (u + 1) * 128] - top)
            total = total + p
            pieces.append(p.astype(BF16))
        lrun[...] = total
        values = kv[pl.ds(pl.multiple_of(n * TILE, TILE), TILE), width : 2 * width]
        acc[...] += jnp.dot(jnp.concatenate(pieces, axis=1), values, preferred_element_type=F32)
        return 0

    lax.fori_loop(0, tiles, weigh, 0)
    total_here = jnp.sum(lrun[...], axis=1, keepdims=True)

    each(nctx, lambda k: count_copy(k).wait_recv())
    added = crecv[0]
    for k in range(1, nctx):
        added = added + crecv[k]
    added = added[0:used]
    before = old_counts[pl.ds(me * used, used), :]
    after = before + added
    diagonal = lax.broadcasted_iota(jnp.int32, (128, 128), 0) == lax.broadcasted_iota(jnp.int32, (128, 128), 1)

    def column(x):
        return jnp.concatenate(
            [jnp.sum(jnp.where(diagonal, x[u : u + 1, :], 0.0), axis=1, keepdims=True) for u in range(used)], axis=0
        )

    before_col, after_col = column(before), column(after)
    for u in range(used):
        out_n[:, u * 128 : (u + 1) * 128] = after[u : u + 1, :]
    log_counts = jnp.log(after) * LOG2E
    centre_bias = []
    for u in range(used):
        per_step = [
            jnp.broadcast_to(hits[s, trows + crows + u : trows + crows + u + 1, :], (copies, 128))
            for s in range(steps)
        ]
        centre_bias.append(jnp.concatenate(per_step, axis=0) + log_counts[u : u + 1, :])
    centre_bias = jnp.concatenate(centre_bias, axis=1)

    loads[4].wait()
    loads[5].wait()
    sibling(7).wait_recv()
    new = []
    for half, out in ((0, out_k), (1, out_v)):
        sums = mixed(7, half, [(0, 3), (1, 3)])
        value = (before_col * cen[half] + sums) / after_col
        out[...] = value
        new.append(value)

    k_high, k_mid, k_low = split3(new[0])
    raw = lax.dot_general(q, k_low, NT, preferred_element_type=F32)
    raw = raw + lax.dot_general(q, k_mid, NT, preferred_element_type=F32)
    raw = raw + lax.dot_general(q, k_high, NT, preferred_element_type=F32)
    centre = ((raw * factor).reshape(nctx, share, owned) + centre_bias[None]).reshape(rows, owned)
    top_centre = jnp.max(centre, axis=1, keepdims=True)
    top = jnp.maximum(top_here, top_centre)
    weights = jnp.exp2(centre - top)
    w_high, w_low = split2(weights)
    v_high, v_low = split2(new[1])
    gathered = jnp.dot(w_low, v_high, preferred_element_type=F32)
    gathered = gathered + jnp.dot(w_high, v_low, preferred_element_type=F32)
    gathered = gathered + jnp.dot(w_high, v_high, preferred_element_type=F32)
    rescale = jnp.exp2(top_here - top)
    whole = jnp.maximum(jnp.sum(weights, axis=1, keepdims=True) + rescale * total_here, 1e-30)
    result = (gathered + rescale * acc[...]) / whole
    lse = top + jnp.log(whole) * LOG2E

    fsend[...] = result.astype(BF16).reshape(nctx, share, width)
    spot = lax.broadcasted_iota(jnp.int32, (rows, 128), 1) == lax.rem(
        lax.broadcasted_iota(jnp.int32, (rows, 128), 0), share
    )
    by_owner = jnp.sum(jnp.where(spot, lse, 0.0).reshape(nctx, share, 128), axis=1)
    for k in range(nctx):
        lsend[k] = by_owner[k : k + 1, :]

    def send(k):
        lse_copy(k).start()
        row_copy(k).start()

    each(nctx, send)
    lrecv[me] = lsend[me]
    frecv[me] = fsend[me]

    each(nctx, lambda k: lse_copy(k).wait_recv())
    logs = jnp.concatenate([lrecv[k] for k in range(nctx)], axis=0)
    factors = jnp.exp2(logs - jnp.max(logs, axis=0, keepdims=True))
    factors = factors / jnp.sum(factors, axis=0, keepdims=True)
    by_row = jnp.transpose(jnp.concatenate([factors, jnp.zeros((128 - nctx, 128), F32)], axis=0))[0:share]
    each(nctx, lambda k: row_copy(k).wait_recv())
    final = jnp.zeros((share, width), F32)
    for k in range(nctx):
        final = final + by_row[:, k : k + 1] * frecv[k].astype(F32)
    out_a[...] = final.astype(BF16)

    for j in range(nz):
        sibling(j).wait_send()
    for copy in hops:
        copy.wait_send()
    each(nhead, lambda k: query_copy(k).wait_send())

    def sent(k):
        count_copy(k).wait_send()
        lse_copy(k).wait_send()
        row_copy(k).wait_send()

    each(nctx, sent)


def shards(
    stretch_keys,
    stretch_values,
    stretch_assign,
    centroid_keys,
    centroid_values,
    cluster_counts,
    cache_keys,
    cache_values,
    block_cluster,
    selected,
    queries,
):
    nctx, nhead = lax.axis_size("ctx"), lax.axis_size("head")
    clusters, width = centroid_keys.shape[1:]
    owned = clusters // nctx
    tokens, cached = stretch_keys.shape[1], cache_keys.shape[1]
    steps, qrows = queries.shape[:2]
    rows = steps * qrows * nhead
    share = rows // nctx
    nz = nctx // 2
    tiles = (tokens + cached) // TILE
    vmem = pl.BlockSpec(memory_space=pltpu.VMEM)
    smem = pl.BlockSpec(memory_space=pltpu.SMEM)
    hbm = pl.BlockSpec(memory_space=pl.ANY)
    dma = pltpu.SemaphoreType.DMA
    new_keys, new_values, new_counts, attended = pl.pallas_call(
        functools.partial(kernel, nctx, nhead, owned, steps, width),
        out_shape=(
            jax.ShapeDtypeStruct((owned, width), F32),
            jax.ShapeDtypeStruct((owned, width), F32),
            jax.ShapeDtypeStruct((1, owned), F32),
            jax.ShapeDtypeStruct((share, width), BF16),
        ),
        in_specs=[smem, vmem, vmem, vmem, vmem] + [hbm] * 6,
        out_specs=(vmem,) * 4,
        scratch_shapes=[
            pltpu.VMEM((tokens + cached, 2 * width), BF16),
            pltpu.VMEM((2, owned, width), F32),
            pltpu.VMEM((steps, (tokens + cached) // 128 + 8, 128), F32),
            pltpu.VMEM((tiles, share, TILE), F32),
            pltpu.VMEM((tiles, rows, TILE), F32),
            pltpu.VMEM((rows, 128), F32),
            pltpu.VMEM((rows, width), F32),
            pltpu.VMEM((rows, 128), F32),
            pltpu.VMEM((2, tokens // 128, 128), F32),
            pltpu.VMEM((2 * owned, 2 * width), F32),
            pltpu.VMEM((nz, owned, 2 * width), F32),
            pltpu.VMEM((nz, owned, 2 * width), BF16),
            pltpu.VMEM((nz, owned, 2 * width), BF16),
            pltpu.VMEM((16, owned, width), BF16),
            pltpu.VMEM((16, owned, width), BF16),
            pltpu.VMEM((nhead, rows // nhead, width), BF16),
            pltpu.VMEM((nhead, rows // nhead, width), BF16),
            pltpu.VMEM((nctx, 8, 128), F32),
            pltpu.VMEM((nctx, 8, 128), F32),
            pltpu.VMEM((nctx, share, width), BF16),
            pltpu.VMEM((nctx, share, width), BF16),
            pltpu.VMEM((nctx, 1, 128), F32),
            pltpu.VMEM((nctx, 1, 128), F32),
            dma((6,)),
            dma((nhead,)), dma((nhead,)), dma((nctx,)), dma((nctx,)), dma((nz,)), dma((nz,)),
            dma((16,)), dma((16,)), dma((nctx,)), dma((nctx,)), dma((nctx,)), dma((nctx,)),
        ],
        compiler_params=pltpu.CompilerParams(
            collective_id=0, has_side_effects=True, vmem_limit_bytes=50 * 1024 * 1024
        ),
        name="retrieve",
    )(
        selected.reshape(steps, selected.shape[2]),
        stretch_assign.reshape(tokens // 128, 128),
        block_cluster,
        cluster_counts.reshape(clusters // 128, 128),
        queries.reshape(rows, width),
        stretch_keys, stretch_values, cache_keys, cache_values, centroid_keys, centroid_values,
    )
    return (
        new_keys[None],
        new_values[None],
        new_counts,
        attended.reshape(steps, 1, share // steps, width),
    )


def solution(mesh):
    in_specs = (
        P("head", "ctx", None),
        P("head", "ctx", None),
        P("head", "ctx"),
        P("head", None, None),
        P("head", None, None),
        P("head", None),
        P("head", "ctx", None),
        P("head", "ctx", None),
        P("head", "ctx"),
        P(None, "head", None),
        P(None, "head", None, None),
    )
    out_specs = (
        P("head", "ctx", None),
        P("head", "ctx", None),
        P("head", "ctx"),
        P(None, "head", "ctx", None),
    )
    return jax.shard_map(shards, mesh=mesh, in_specs=in_specs, out_specs=out_specs, check_vma=False)
```

time: 182 us -> 57.7 us (0.32)
  waiting for transfers between devices: 51.6 us -> 0 us
  Pallas kernels: 0 us -> 48.1 us
  other arithmetic: 43.3 us -> 0 us
  starting transfers between devices: 21.6 us -> 0 us
  matrix products: 20.8 us -> 0 us
  local copies, waits for them, and re-layouts: 25.6 us -> 8.54 us
  blocking collectives: 16.9 us -> 0 us
    all_to_all x3 -> x0, waiting for transfers between devices: 51.6 us -> none  [the longest x1 45.7 us: shards(): lax.all_to_all(buffer, 'ctx', split_axis=1, concat_axis=1, tiled=True)]
    pallas_call x0 -> x1, Pallas kernels: none -> 48.1 us  [shards(): pl.pallas_call(functools.partial(kernel, nctx, nhead, owned, steps, width...]
    all_to_all x3 -> x0, starting transfers between devices: 21.6 us -> none  [the longest x1 9.98 us: shards(): lax.all_to_all(marks, 'ctx', split_axis=1, concat_axis=1, tiled=True)]
    unnamed x5 -> x0, other arithmetic: 21.6 us -> none
    dot_general x7 -> x0, matrix products: 20.8 us -> none  [the longest x1 5.64 us: shards(): jnp.einsum('htc,htd->hcd', owner_hits.astype(jnp.bfloat16), arrived, pref...]
    all_to_all x1 -> x0, blocking collectives: 16.9 us -> none  [in_one_piece(): lax.all_to_all(both, axis, split_axis=split_dim, concat_axis=concat_dim,...]
    unnamed x41 -> x18, local copies, waits for them, and re-layouts: 18.8 us -> 8.54 us
    another operation x2 -> x0, other arithmetic: 8.48 us -> none
  transfers between devices with their start and end apart: 3 -> 0, of which waited for: 2 -> 0; matrix products, arithmetic and copies ran while one was open for 20% -> 0% of each run, Pallas kernels for 0% -> 0%
where the time goes in v1:
time: 57.7 us; the launch traced here: 57.3 us
  Pallas kernels  48.1 us (83%)
  local copies, waits for them, and re-layouts  8.54 us (15%)
  between operations  0.66 us (1%)
    pallas_call x1, Pallas kernels, shards(): pl.pallas_call(functools.partial(kernel, nctx, nhead, owned, steps, width...  48.1 us
    unnamed x18, local copies, waits for them, and re-layouts  8.54 us

profile of v1, /device:TPU:1, one launch (start us, length us, event | category | flops | bytes accessed | tf_op | source)
XLA Modules:
  0.0 57.3 jit_solution(7949832606893218610)
XLA Ops:
  0.6 0.0 copy-start
  0.6 1.2 %copy-done = bf16[1,4096,128]{2,1,0:T(8,128)(2,1)S(1)} copy-done((bf16[1,4096,128]{2,1,0:T(8,128)(2,1)S(1)}, bf16[1,4096,128]{2,1,0:T(8,128)(2,1)}, u32[]{:S(2)}) %copy-start) | copy-done | bytes 1048600
  1.9 0.0 copy-start.1
  1.9 1.2 %copy-done.1 = bf16[1,4096,128]{2,1,0:T(8,128)(2,1)S(1)} copy-done((bf16[1,4096,128]{2,1,0:T(8,128)(2,1)S(1)}, bf16[1,4096,128]{2,1,0:T(8,128)(2,1)}, u32[]{:S(2)}) %copy-start.1) | copy-done | bytes 1048600
  3.1 0.0 copy-start.2
  3.1 0.8 %copy-done.2 = bf16[4,4,16,128]{3,2,1,0:T(8,128)(2,1)S(1)} copy-done((bf16[4,4,16,128]{3,2,1,0:T(8,128)(2,1)S(1)}, bf16[4,4,16,128]{3,2,1,0:T(8,128)(2,1)}, u32[]{:S(2)}) %copy-start.2) | copy-done | bytes 65560
  3.9 0.0 copy-start.3
  3.9 0.7 %copy-done.3 = s32[1,4096]{1,0:T(1,128)S(1)} copy-done((s32[1,4096]{1,0:T(1,128)S(1)}, s32[1,4096]{1,0:T(1,128)}, u32[]{:S(2)}) %copy-start.3) | copy-done | bytes 16408
  4.6 0.0 copy-start.4
  4.6 0.7 %copy-done.4 = f32[1,4096]{1,0:T(1,128)S(1)} copy-done((f32[1,4096]{1,0:T(1,128)S(1)}, f32[1,4096]{1,0:T(1,128)}, u32[]{:S(2)}) %copy-start.4) | copy-done | bytes 16408
  5.4 0.0 copy-start.5
  5.4 0.7 %copy-done.5 = s32[4,1,64]{2,1,0:T(1,128)S(1)} copy-done((s32[4,1,64]{2,1,0:T(1,128)S(1)}, s32[4,1,64]{2,1,0:T(1,128)}, u32[]{:S(2)}) %copy-start.5) | copy-done | bytes 1048
  6.0 0.0 copy-start.6
  6.0 0.7 %copy-done.6 = s32[1,512]{1,0:T(1,128)S(1)} copy-done((s32[1,512]{1,0:T(1,128)S(1)}, s32[1,512]{1,0:T(1,128)}, u32[]{:S(2)}) %copy-start.6) | copy-done | bytes 2072
  6.7 48.1 %retrieve.1 = (f32[256,128]{1,0:T(8,128)S(1)}, f32[256,128]{1,0:T(8,128)S(1)}, f32[1,256]{1,0:T(1,128)S(1)}, bf16[16,128]{1,0:T(8,128)(2,1)S(1)}) custom-call(s32[4,64]{1,0:T(4,128)S(1)} %bitcast.15, s32[32,128]{1,0:T(8,128)S(1)} %bitcast.12, s32[1,512]{1,0:T(1,128)S(1)} %copy-done.6, f32[32,128]{1,0:T(8,128)S(1)} %bitcast.13, ...), custom_call_target="tpu_custom_call" | custom-call | tf_op jit(solution)/shard_map/retrieve/pallas_call | solution.py:444
  54.9 0.7 %copy.20 = f32[1,256,128]{2,1,0:T(8,128)} copy(f32[1,256,128]{2,1,0:T(8,128)S(1)} %bitcast.10) | data formatting | bytes 262144
  55.5 0.7 %copy.21 = f32[1,256,128]{2,1,0:T(8,128)} copy(f32[1,256,128]{2,1,0:T(8,128)S(1)} %bitcast.9) | data formatting | bytes 262144
  56.2 0.6 copy.22
  56.8 0.6 %copy.23 = bf16[4,1,4,128]{3,2,1,0:T(4,128)(2,1)} copy(bf16[4,1,4,128]{3,2,1,0:T(4,128)(2,1)S(1)} %bitcast.14) | data formatting | bytes 8192
Async XLA Ops:
  0.6 1.2 %copy-start = (bf16[1,4096,128]{2,1,0:T(8,128)(2,1)S(1)}, bf16[1,4096,128]{2,1,0:T(8,128)(2,1)}, u32[]{:S(2)}) copy-start(bf16[1,4096,128]{2,1,0:T(8,128)(2,1)} %skeys.1) | copy-start | bytes 3145732
  1.9 1.2 %copy-start.1 = (bf16[1,4096,128]{2,1,0:T(8,128)(2,1)S(1)}, bf16[1,4096,128]{2,1,0:T(8,128)(2,1)}, u32[]{:S(2)}) copy-start(bf16[1,4096,128]{2,1,0:T(8,128)(2,1)} %svals.1) | copy-start | bytes 3145732
  3.1 0.8 %copy-start.2 = (bf16[4,4,16,128]{3,2,1,0:T(8,128)(2,1)S(1)}, bf16[4,4,16,128]{3,2,1,0:T(8,128)(2,1)}, u32[]{:S(2)}) copy-start(bf16[4,4,16,128]{3,2,1,0:T(8,128)(2,1)} %param.21) | copy-start | bytes 196612
  3.9 0.7 %copy-start.3 = (s32[1,4096]{1,0:T(1,128)S(1)}, s32[1,4096]{1,0:T(1,128)}, u32[]{:S(2)}) copy-start(s32[1,4096]{1,0:T(1,128)} %param.13) | copy-start | bytes 49156
  4.6 0.7 %copy-start.4 = (f32[1,4096]{1,0:T(1,128)S(1)}, f32[1,4096]{1,0:T(1,128)}, u32[]{:S(2)}) copy-start(f32[1,4096]{1,0:T(1,128)} %param.16) | copy-start | bytes 49156
  5.4 0.7 %copy-start.5 = (s32[4,1,64]{2,1,0:T(1,128)S(1)}, s32[4,1,64]{2,1,0:T(1,128)}, u32[]{:S(2)}) copy-start(s32[4,1,64]{2,1,0:T(1,128)} %param.20) | copy-start | bytes 3076
  6.0 0.7 %copy-start.6 = (s32[1,512]{1,0:T(1,128)S(1)}, s32[1,512]{1,0:T(1,128)}, u32[]{:S(2)}) copy-start(s32[1,512]{1,0:T(1,128)} %blocks.1) | copy-start | bytes 6148

commit v2 on v1

--- a/solution.py
+++ b/solution.py
@@ -14,8 +14,7 @@
 LOG2E = math.log2(math.e)
 MASKED = -1e30
 FLOOR = -1e29
-TILE = 512
-SEG = 1024
+TILE = 2048
 NT = (((1,), (1,)), ((), ()))
 
 
@@ -33,9 +32,9 @@
 
 def kernel(
     nctx, nhead, owned, steps, width,
-    sel, assign, blocks, old_counts, queries, skeys, svals, ckeys, cvals, cent_k, cent_v,
+    sel_in, assign_in, blocks_in, counts_in, queries_in, skeys, svals, ckeys, cvals, cent_k, cent_v,
     out_k, out_v, out_n, out_a,
-    kv, cen, hits, bias, scores, mrun, acc, lrun, rel, part, own,
+    sel, assign, blocks, old_counts, queries, kv, cen, hits, bias, scores, mrun, acc, lrun, rel, own,
     sib_send, sib_recv, ring_send, ring_recv, qsend, qrecv, csend, crecv, fsend, frecv, lsend, lrecv,
     load_sem, q_ss, q_rs, c_ss, c_rs, s_ss, s_rs, r_ss, r_rs, f_ss, f_rs, l_ss, l_rs,
 ):
@@ -45,7 +44,7 @@
     nz = nctx // 2
     tokens = skeys.shape[1]
     cached = ckeys.shape[1]
-    rows = queries.shape[0]
+    rows = queries_in.shape[0]
     share = rows // nctx
     stretch_tiles = tokens // TILE
     tiles = (tokens + cached) // TILE
@@ -58,7 +57,16 @@
         pltpu.make_async_copy(cent_k.at[0, pl.ds(me * owned, owned), :], cen.at[0], load_sem.at[4]),
         pltpu.make_async_copy(cent_v.at[0, pl.ds(me * owned, owned), :], cen.at[1], load_sem.at[5]),
     ]
-    for load in loads:
+    small = [
+        pltpu.make_async_copy(source, target, load_sem.at[6 + n])
+        for n, (source, target) in enumerate(
+            ((assign_in, assign), (queries_in, queries), (sel_in, sel), (blocks_in, blocks), (counts_in, old_counts))
+        )
+    ]
+    small[0].start()
+    loads[0].start()
+    loads[1].start()
+    for load in small[1:] + loads[2:]:
         load.start()
 
     barrier = pltpu.get_barrier_semaphore()
@@ -74,6 +82,7 @@
     lax.fori_loop(1, nctx, greet, 0)
     lax.fori_loop(1, nhead, greet_heads, 0)
 
+    small[0].wait()
     ids = assign[...]
 
     iota = lax.broadcasted_iota(jnp.int32, (owned, width), 0).astype(F32).astype(BF16)
@@ -83,26 +92,17 @@
         zd = lax.rem(z + offset, nz)
         rel[0] = (ids - owned * (2 * zd + 1 - core)).astype(F32)
         rel[1] = (ids - owned * (2 * zd + core)).astype(F32)
-        part[...] = jnp.zeros_like(part)
-
-        def step(n, _):
-            hot = []
-            for side in range(2):
-                block = rel[side, pl.ds(pl.multiple_of(n * (SEG // 128), 8), SEG // 128), :]
-                pieces = []
-                for u in range(SEG // 128):
-                    row = jnp.broadcast_to(block[u : u + 1, :], (16, 128)).astype(BF16)
-                    equal = iota == row[None]
-                    pieces.append(jnp.where(equal, jnp.ones((), BF16), jnp.zeros((), BF16)).reshape(owned, 128))
-                hot.append(jnp.concatenate(pieces, axis=1))
-            hot = jnp.concatenate(hot, axis=0)
-            data = kv[pl.ds(pl.multiple_of(n * SEG, SEG), SEG), :]
-            part[...] += jnp.dot(hot, data, preferred_element_type=F32)
-            return 0
-
-        lax.fori_loop(0, tokens // SEG, step, 0)
-        sib_send[j] = part[0:owned, :].astype(BF16)
-        own[j] = part[owned : 2 * owned, :]
+        hot = []
+        for side in range(2):
+            pieces = []
+            for u in range(tokens // 128):
+                row = jnp.broadcast_to(rel[side, u : u + 1, :], (16, 128)).astype(BF16)
+                equal = iota == row[None]
+                pieces.append(jnp.where(equal, jnp.ones((), BF16), jnp.zeros((), BF16)).reshape(owned, 128))
+            hot.append(jnp.concatenate(pieces, axis=1))
+        sums = jnp.dot(jnp.concatenate(hot, axis=0), kv[0:tokens, :], preferred_element_type=F32)
+        sib_send[j] = sums[0:owned].astype(BF16)
+        own[j] = sums[owned : 2 * owned]
 
     def sibling(j):
         return pltpu.make_async_remote_copy(
@@ -183,6 +183,7 @@
     r_in = lax.broadcasted_iota(jnp.int32, (rows, rows), 1)
     per = rows // nhead
     order = jnp.where(r_in == lax.rem(r_out, per) * nhead + r_out // per, 1.0, 0.0).astype(BF16)
+    small[1].wait()
     qsend[...] = jnp.dot(order, queries[...], preferred_element_type=F32).astype(BF16).reshape(nhead, per, width)
 
     loads[0].wait()
@@ -205,27 +206,23 @@
     lanes = lax.broadcasted_iota(jnp.int32, (128, 128), 0).astype(F32).astype(BF16).reshape(8, 16, 128)
     rel[0] = lax.shift_right_logical(ids, 7).astype(F32)
     rel[1] = (ids & 127).astype(F32)
-    part[0 : nctx * 8, 0:128] = jnp.zeros((nctx * 8, 128), F32)
-
-    def count_step(n, _):
-        both = []
-        for side, table in ((0, pattern), (1, lanes)):
-            block = rel[side, pl.ds(pl.multiple_of(n * (SEG // 128), 8), SEG // 128), :]
-            pieces = []
-            for u in range(SEG // 128):
-                row = jnp.broadcast_to(block[u : u + 1, :], (16, 128)).astype(BF16)
-                equal = table == row[None]
-                pieces.append(jnp.where(equal, jnp.ones((), BF16), jnp.zeros((), BF16)).reshape(-1, 128))
-            both.append(jnp.concatenate(pieces, axis=1))
-        part[0 : nctx * 8, 0:128] += lax.dot_general(both[0], both[1], NT, preferred_element_type=F32)
-        return 0
-
-    lax.fori_loop(0, tokens // SEG, count_step, 0)
-    csend[...] = part[0 : nctx * 8, 0:128].reshape(nctx, 8, 128)
+    both = []
+    for side, table in ((0, pattern), (1, lanes)):
+        pieces = []
+        for u in range(tokens // 128):
+            row = jnp.broadcast_to(rel[side, u : u + 1, :], (16, 128)).astype(BF16)
+            equal = table == row[None]
+            pieces.append(jnp.where(equal, jnp.ones((), BF16), jnp.zeros((), BF16)).reshape(-1, 128))
+        both.append(jnp.concatenate(pieces, axis=1))
+    named = lax.dot_general(both[0], both[1], NT, preferred_element_type=F32)
+    csend[...] = named.reshape(nctx, 8, 128)
     each(nctx, lambda k: count_copy(k).start())
     crecv[me] = csend[me]
 
     nblk = blocks.shape[1]
+    small[2].wait()
+    small[3].wait()
+    small[4].wait()
     lane = lax.broadcasted_iota(jnp.int32, (16, 128), 1)
     sub = lax.broadcasted_iota(jnp.int32, (16, 128), 0)
     spread = sub * 8 + lane // 16
@@ -438,8 +435,7 @@
     nz = nctx // 2
     tiles = (tokens + cached) // TILE
     vmem = pl.BlockSpec(memory_space=pltpu.VMEM)
-    smem = pl.BlockSpec(memory_space=pltpu.SMEM)
-    hbm = pl.BlockSpec(memory_space=pl.ANY)
+    hbm = pl.BlockSpec(memory_space=pltpu.HBM)
     dma = pltpu.SemaphoreType.DMA
     new_keys, new_values, new_counts, attended = pl.pallas_call(
         functools.partial(kernel, nctx, nhead, owned, steps, width),
@@ -449,9 +445,14 @@
             jax.ShapeDtypeStruct((1, owned), F32),
             jax.ShapeDtypeStruct((share, width), BF16),
         ),
-        in_specs=[smem, vmem, vmem, vmem, vmem] + [hbm] * 6,
+        in_specs=[hbm] * 11,
         out_specs=(vmem,) * 4,
         scratch_shapes=[
+            pltpu.SMEM((steps, selected.shape[2]), jnp.int32),
+            pltpu.VMEM((tokens // 128, 128), jnp.int32),
+            pltpu.VMEM(block_cluster.shape, jnp.int32),
+            pltpu.VMEM((clusters // 128, 128), F32),
+            pltpu.VMEM((rows, width), BF16),
             pltpu.VMEM((tokens + cached, 2 * width), BF16),
             pltpu.VMEM((2, owned, width), F32),
             pltpu.VMEM((steps, (tokens + cached) // 128 + 8, 128), F32),
@@ -461,7 +462,6 @@
             pltpu.VMEM((rows, width), F32),
             pltpu.VMEM((rows, 128), F32),
             pltpu.VMEM((2, tokens // 128, 128), F32),
-            pltpu.VMEM((2 * owned, 2 * width), F32),
             pltpu.VMEM((nz, owned, 2 * width), F32),
             pltpu.VMEM((nz, owned, 2 * width), BF16),
             pltpu.VMEM((nz, owned, 2 * width), BF16),
@@ -475,12 +475,12 @@
             pltpu.VMEM((nctx, share, width), BF16),
             pltpu.VMEM((nctx, 1, 128), F32),
             pltpu.VMEM((nctx, 1, 128), F32),
-            dma((6,)),
+            dma((11,)),
             dma((nhead,)), dma((nhead,)), dma((nctx,)), dma((nctx,)), dma((nz,)), dma((nz,)),
             dma((16,)), dma((16,)), dma((nctx,)), dma((nctx,)), dma((nctx,)), dma((nctx,)),
         ],
         compiler_params=pltpu.CompilerParams(
-            collective_id=0, has_side_effects=True, vmem_limit_bytes=50 * 1024 * 1024
+            collective_id=0, has_side_effects=True, vmem_limit_bytes=60000000
         ),
         name="retrieve",
     )(

time: 57.7 us -> 50.8 us (0.88)
  Pallas kernels: 48.1 us -> 44.3 us
  local copies, waits for them, and re-layouts: 8.54 us -> 5.64 us
    pallas_call x1, Pallas kernels: 48.1 us -> 44.3 us  [shards(): pl.pallas_call(functools.partial(kernel, nctx, nhead, owned, steps, width...]
    unnamed x18 -> x4, local copies, waits for them, and re-layouts: 8.54 us -> 5.64 us
where the time goes in v2:
time: 50.8 us; the launch traced here: 50.6 us
  Pallas kernels  44.3 us (87%)
  local copies, waits for them, and re-layouts  5.64 us (11%)
  between operations  0.64 us (1%)
    pallas_call x1, Pallas kernels, shards(): pl.pallas_call(functools.partial(kernel, nctx, nhead, owned, steps, width...  44.3 us
    unnamed x4, local copies, waits for them, and re-layouts  5.64 us

profile of v2, /device:TPU:1, one launch (start us, length us, event | category | flops | bytes accessed | tf_op | source)
XLA Modules:
  0.0 50.6 jit_solution(13779425437684858766)
XLA Ops:
  0.6 44.3 %retrieve.1 = (f32[256,128]{1,0:T(8,128)}, f32[256,128]{1,0:T(8,128)}, f32[1,256]{1,0:T(1,128)}, bf16[16,128]{1,0:T(8,128)(2,1)}) custom-call(s32[4,64]{1,0:T(4,128)} %bitcast.15, s32[32,128]{1,0:T(8,128)} %bitcast.12, s32[1,512]{1,0:T(1,128)} %blocks_in.1, f32[32,128]{1,0:T(8,128)} %bitcast.13, bf16[256,128]{1,0:T(8,128)(2,1)} %bitcast.11, ...), custom_call_target="tpu_custom_call" | custom-call | tf_op jit(solution)/shard_map/retrieve/pallas_call | solution.py:440
  44.9 1.6 %copy.20 = f32[1,256,128]{2,1,0:T(8,128)} copy(f32[1,256,128]{2,1,0:T(8,128)} %bitcast.10) | data formatting | bytes 262144
  46.5 1.6 %copy.21 = f32[1,256,128]{2,1,0:T(8,128)} copy(f32[1,256,128]{2,1,0:T(8,128)} %bitcast.9) | data formatting | bytes 262144
  48.1 1.2 %copy.22 = f32[1,256]{1,0:T(1,128)} copy(f32[1,256]{1,0:T(1,128)} %get-tuple-element.22) | data formatting | bytes 2048
  49.3 1.3 %copy.23 = bf16[4,1,4,128]{3,2,1,0:T(4,128)(2,1)} copy(bf16[4,1,4,128]{3,2,1,0:T(4,128)(2,1)} %bitcast.14) | data formatting | bytes 8192

commit v3 on v2

--- a/solution.py
+++ b/solution.py
@@ -35,8 +35,8 @@
     sel_in, assign_in, blocks_in, counts_in, queries_in, skeys, svals, ckeys, cvals, cent_k, cent_v,
     out_k, out_v, out_n, out_a,
     sel, assign, blocks, old_counts, queries, kv, cen, hits, bias, scores, mrun, acc, lrun, rel, own,
-    sib_send, sib_recv, ring_send, ring_recv, qsend, qrecv, csend, crecv, fsend, frecv, lsend, lrecv,
-    load_sem, q_ss, q_rs, c_ss, c_rs, s_ss, s_rs, r_ss, r_rs, f_ss, f_rs, l_ss, l_rs,
+    sib_send, sib_recv, ring_send, ring_recv, qsend, qrecv, named, fsend, frecv,
+    load_sem, q_ss, q_rs, s_ss, s_rs, r_ss, r_rs, f_ss, f_rs,
 ):
     me = lax.axis_index("ctx")
     head = lax.axis_index("head")
@@ -87,6 +87,14 @@
 
     iota = lax.broadcasted_iota(jnp.int32, (owned, width), 0).astype(F32).astype(BF16)
     iota = iota.reshape(owned // 16, 16, width)
+
+    def counts_out(value):
+        high = jnp.floor(value * (1 / 256))
+        return jnp.concatenate([value - 256 * high, high], axis=0).astype(BF16)
+
+    def counts_in(tile):
+        tile = tile.astype(F32)
+        return tile[0:8] + 256 * tile[8:16]
 
     def segment(j, offset):
         zd = lax.rem(z + offset, nz)
@@ -101,8 +109,13 @@
                 pieces.append(jnp.where(equal, jnp.ones((), BF16), jnp.zeros((), BF16)).reshape(owned, 128))
             hot.append(jnp.concatenate(pieces, axis=1))
         sums = jnp.dot(jnp.concatenate(hot, axis=0), kv[0:tokens, :], preferred_element_type=F32)
-        sib_send[j] = sums[0:owned].astype(BF16)
+        sib_send[j, 0:owned, :] = sums[0:owned].astype(BF16)
+        sib_send[j, owned:, 0:width] = counts_out(named[2 * zd + 1 - core])
+        sib_send[j, owned:, width:] = jnp.zeros((16, width), BF16)
         own[j] = sums[owned : 2 * owned]
+        if j == 0:
+            pl.semaphore_wait(barrier, nctx - 1 + nhead - 1)
+        sibling(j).start()
 
     def sibling(j):
         return pltpu.make_async_remote_copy(
@@ -113,63 +126,74 @@
     def hop(direction, step, half):
         at = (direction * 4 + step) * 2 + half
         to = lax.rem(z + (1 if direction == 0 else nz - 1), nz)
+        length = owned + (16 if half == 0 else 0)
         return pltpu.make_async_remote_copy(
-            ring_send.at[at], ring_recv.at[at], r_ss.at[at], r_rs.at[at],
+            ring_send.at[at, pl.ds(0, length), :], ring_recv.at[at, pl.ds(0, length), :], r_ss.at[at], r_rs.at[at],
             device_id={"ctx": 2 * to + core}, device_id_type=MESH,
         )
 
-    def mixed(j, half, arrivals):
+    def mixed(j, offset, half, arrivals):
         columns = slice(half * width, (half + 1) * width)
-        value = own[j, :, columns] + sib_recv[j, :, columns].astype(F32)
+        value = own[j, :, columns] + sib_recv[j, 0:owned, columns].astype(F32)
+        count = None
+        if half == 0:
+            count = named[2 * lax.rem(z + offset, nz) + core] + counts_in(sib_recv[j, owned:, 0:width])
         for direction, step in arrivals:
             hop(direction, step, half).wait_recv()
-            value = value + ring_recv[(direction * 4 + step) * 2 + half].astype(F32)
-        return value
+            at = (direction * 4 + step) * 2 + half
+            value = value + ring_recv[at, 0:owned, :].astype(F32)
+            if half == 0:
+                count = count + counts_in(ring_recv[at, owned:, :])
+        return value, count
 
     hops = []
 
-    def forward(j, direction, step):
+    def launch(j, offset, direction, step, half, arrivals):
+        at = (direction * 4 + step) * 2 + half
+        value, count = mixed(j, offset, half, arrivals)
+        ring_send[at, 0:owned, :] = value.astype(BF16)
+        if half == 0:
+            ring_send[at, owned:, :] = counts_out(count)
+        copy = hop(direction, step, half)
+        copy.start()
+        hops.append(copy)
+
+    def forward(j, offset, direction, step):
         sibling(j).wait_recv()
         first = 0 if direction == 0 else 1
         for half in (first, 1 - first):
             arrivals = []
             if step >= 2 or (step == 1 and half == first):
                 arrivals = [(direction, step - 1)]
-            ring_send[(direction * 4 + step) * 2 + half] = mixed(j, half, arrivals).astype(BF16)
-            copy = hop(direction, step, half)
-            copy.start()
-            hops.append(copy)
+            launch(j, offset, direction, step, half, arrivals)
 
     def start_ring():
         sibling(0).wait_recv()
         for direction in (0, 1):
-            ring_send[direction * 8 + direction] = mixed(0, direction, []).astype(BF16)
-            copy = hop(direction, 0, direction)
-            copy.start()
-            hops.append(copy)
+            launch(0, 4, direction, 0, direction, [])
 
     def query_copy(k):
         to = lax.rem(head + k, nhead)
         return pltpu.make_async_remote_copy(
-            qsend.at[to], qrecv.at[head], q_ss.at[k], q_rs.at[k], device_id={"head": to}, device_id_type=MESH
-        )
-
-    def count_copy(k):
-        to = lax.rem(me + k, nctx)
-        return pltpu.make_async_remote_copy(
-            csend.at[to], crecv.at[me], c_ss.at[k], c_rs.at[k], device_id={"ctx": to}, device_id_type=MESH
+            qsend.at[to], qrecv.at[head], q_ss, q_rs, device_id={"head": to}, device_id_type=MESH
         )
 
     def row_copy(k):
         to = lax.rem(me + k, nctx)
         return pltpu.make_async_remote_copy(
-            fsend.at[to], frecv.at[me], f_ss.at[k], f_rs.at[k], device_id={"ctx": to}, device_id_type=MESH
-        )
-
-    def lse_copy(k):
-        to = lax.rem(me + k, nctx)
+            fsend.at[to], frecv.at[me], f_ss, f_rs, device_id={"ctx": to}, device_id_type=MESH
+        )
+
+    def all_queries():
+        part = pl.ds(0, nhead - 1)
         return pltpu.make_async_remote_copy(
-            lsend.at[to], lrecv.at[me], l_ss.at[k], l_rs.at[k], device_id={"ctx": to}, device_id_type=MESH
+            qsend.at[part], qrecv.at[part], q_ss, q_rs, device_id={"head": lax.rem(head + 1, nhead)}, device_id_type=MESH
+        )
+
+    def all_rows():
+        part = pl.ds(0, nctx - 1)
+        return pltpu.make_async_remote_copy(
+            fsend.at[part], frecv.at[part], f_ss, f_rs, device_id={"ctx": lax.rem(me + 1, nctx)}, device_id_type=MESH
         )
 
     def each(count, act):
@@ -178,26 +202,6 @@
             return 0
 
         lax.fori_loop(1, count, step, 0)
-
-    r_out = lax.broadcasted_iota(jnp.int32, (rows, rows), 0)
-    r_in = lax.broadcasted_iota(jnp.int32, (rows, rows), 1)
-    per = rows // nhead
-    order = jnp.where(r_in == lax.rem(r_out, per) * nhead + r_out // per, 1.0, 0.0).astype(BF16)
-    small[1].wait()
-    qsend[...] = jnp.dot(order, queries[...], preferred_element_type=F32).astype(BF16).reshape(nhead, per, width)
-
-    loads[0].wait()
-    loads[1].wait()
-    segment(0, 4)
-    pl.semaphore_wait(barrier, nctx - 1 + nhead - 1)
-    sibling(0).start()
-    each(nhead, lambda k: query_copy(k).start())
-    qrecv[head] = qsend[head]
-    segment(1, 3)
-    sibling(1).start()
-    start_ring()
-    segment(2, 5)
-    sibling(2).start()
 
     used = owned // 128
     r = lax.broadcasted_iota(jnp.int32, (nctx * 8, 128), 0)
@@ -214,10 +218,24 @@
             equal = table == row[None]
             pieces.append(jnp.where(equal, jnp.ones((), BF16), jnp.zeros((), BF16)).reshape(-1, 128))
         both.append(jnp.concatenate(pieces, axis=1))
-    named = lax.dot_general(both[0], both[1], NT, preferred_element_type=F32)
-    csend[...] = named.reshape(nctx, 8, 128)
-    each(nctx, lambda k: count_copy(k).start())
-    crecv[me] = csend[me]
+    tally = lax.dot_general(both[0], both[1], NT, preferred_element_type=F32)
+    named[...] = tally.reshape(nctx, 8, 128)
+
+    r_out = lax.broadcasted_iota(jnp.int32, (rows, rows), 0)
+    r_in = lax.broadcasted_iota(jnp.int32, (rows, rows), 1)
+    per = rows // nhead
+    order = jnp.where(r_in == lax.rem(r_out, per) * nhead + r_out // per, 1.0, 0.0).astype(BF16)
+    small[1].wait()
+    qsend[...] = jnp.dot(order, queries[...], preferred_element_type=F32).astype(BF16).reshape(nhead, per, width)
+
+    loads[0].wait()
+    loads[1].wait()
+    segment(0, 4)
+    each(nhead, lambda k: query_copy(k).start())
+    qrecv[head] = qsend[head]
+    segment(1, 3)
+    start_ring()
+    segment(2, 5)
 
     nblk = blocks.shape[1]
     small[2].wait()
@@ -256,15 +274,13 @@
 
     lax.fori_loop(0, tiles, spread_bias, 0)
 
-    forward(1, 0, 1)
-    forward(2, 1, 1)
+    forward(1, 3, 0, 1)
+    forward(2, 5, 1, 1)
 
     segment(3, 2)
-    sibling(3).start()
     segment(4, 6)
-    sibling(4).start()
-
-    each(nhead, lambda k: query_copy(k).wait_recv())
+
+    all_queries().wait_recv()
     q = qrecv[...].reshape(rows, width)
     factor = width**-0.5 * LOG2E
     mrun[...] = jnp.full(mrun.shape, FLOOR, F32)
@@ -284,17 +300,14 @@
     loads[3].wait()
     lax.fori_loop(0, tiles // 2, score, 0)
 
-    forward(3, 0, 2)
-    forward(4, 1, 2)
+    forward(3, 2, 0, 2)
+    forward(4, 6, 1, 2)
     segment(5, 1)
-    sibling(5).start()
     segment(6, 7)
-    sibling(6).start()
     lax.fori_loop(tiles // 2, tiles, score, 0)
-    forward(5, 0, 3)
-    forward(6, 1, 3)
+    forward(5, 1, 0, 3)
+    forward(6, 7, 1, 3)
     segment(7, 0)
-    sibling(7).start()
 
     top_here = jnp.max(mrun[...], axis=1, keepdims=True)
     mrun[...] = jnp.broadcast_to(top_here, mrun.shape)
@@ -316,10 +329,12 @@
     lax.fori_loop(0, tiles, weigh, 0)
     total_here = jnp.sum(lrun[...], axis=1, keepdims=True)
 
-    each(nctx, lambda k: count_copy(k).wait_recv())
-    added = crecv[0]
-    for k in range(1, nctx):
-        added = added + crecv[k]
+    loads[4].wait()
+    loads[5].wait()
+    sibling(7).wait_recv()
+    ends = [(0, 3), (1, 3)]
+    key_sums, added = mixed(7, 0, 0, ends)
+    value_sums, _ = mixed(7, 0, 1, ends)
     added = added[0:used]
     before = old_counts[pl.ds(me * used, used), :]
     after = before + added
@@ -343,12 +358,8 @@
         centre_bias.append(jnp.concatenate(per_step, axis=0) + log_counts[u : u + 1, :])
     centre_bias = jnp.concatenate(centre_bias, axis=1)
 
-    loads[4].wait()
-    loads[5].wait()
-    sibling(7).wait_recv()
     new = []
-    for half, out in ((0, out_k), (1, out_v)):
-        sums = mixed(7, half, [(0, 3), (1, 3)])
+    for half, out, sums in ((0, out_k, key_sums), (1, out_v, value_sums)):
         value = (before_col * cen[half] + sums) / after_col
         out[...] = value
         new.append(value)
@@ -371,45 +382,29 @@
     result = (gathered + rescale * acc[...]) / whole
     lse = top + jnp.log(whole) * LOG2E
 
-    fsend[...] = result.astype(BF16).reshape(nctx, share, width)
-    spot = lax.broadcasted_iota(jnp.int32, (rows, 128), 1) == lax.rem(
-        lax.broadcasted_iota(jnp.int32, (rows, 128), 0), share
-    )
-    by_owner = jnp.sum(jnp.where(spot, lse, 0.0).reshape(nctx, share, 128), axis=1)
-    for k in range(nctx):
-        lsend[k] = by_owner[k : k + 1, :]
-
-    def send(k):
-        lse_copy(k).start()
-        row_copy(k).start()
-
-    each(nctx, send)
-    lrecv[me] = lsend[me]
+    fsend[:, 0:share, :] = result.astype(BF16).reshape(nctx, share, width)
+    spot = lax.broadcasted_iota(jnp.int32, (rows, 128), 1)
+    high, mid, low = (x.astype(F32) for x in split3(lse))
+    three = jnp.where(spot == 0, high, jnp.where(spot == 1, mid, jnp.where(spot == 2, low, 0.0)))
+    fsend[:, share:, :] = three.astype(BF16).reshape(nctx, share, 128)
+    each(nctx, lambda k: row_copy(k).start())
     frecv[me] = fsend[me]
-
-    each(nctx, lambda k: lse_copy(k).wait_recv())
-    logs = jnp.concatenate([lrecv[k] for k in range(nctx)], axis=0)
-    factors = jnp.exp2(logs - jnp.max(logs, axis=0, keepdims=True))
-    factors = factors / jnp.sum(factors, axis=0, keepdims=True)
-    by_row = jnp.transpose(jnp.concatenate([factors, jnp.zeros((128 - nctx, 128), F32)], axis=0))[0:share]
-    each(nctx, lambda k: row_copy(k).wait_recv())
-    final = jnp.zeros((share, width), F32)
-    for k in range(nctx):
-        final = final + by_row[:, k : k + 1] * frecv[k].astype(F32)
-    out_a[...] = final.astype(BF16)
-
+    for copy in hops:
+        copy.wait_send()
     for j in range(nz):
         sibling(j).wait_send()
-    for copy in hops:
-        copy.wait_send()
-    each(nhead, lambda k: query_copy(k).wait_send())
-
-    def sent(k):
-        count_copy(k).wait_send()
-        lse_copy(k).wait_send()
-        row_copy(k).wait_send()
-
-    each(nctx, sent)
+    all_queries().wait_send()
+    all_rows().wait_recv()
+    logs = jnp.sum(frecv[:, share:, :].astype(F32), axis=2, keepdims=True)
+    factors = jnp.exp2(logs - jnp.max(logs, axis=0, keepdims=True))
+    final = jnp.sum(factors * frecv[:, 0:share, :].astype(F32), axis=0) / jnp.sum(factors, axis=0)
+    out_a[...] = final.astype(BF16)
+    all_rows().wait_send()
+
+
+def finish_kernel(k_in, v_in, n_in, a_in, k_out, v_out, n_out, a_out):
+    for source, target in ((k_in, k_out), (v_in, v_out), (n_in, n_out), (a_in, a_out)):
+        target[...] = source[...]
 
 
 def shards(
@@ -437,14 +432,15 @@
     vmem = pl.BlockSpec(memory_space=pltpu.VMEM)
     hbm = pl.BlockSpec(memory_space=pltpu.HBM)
     dma = pltpu.SemaphoreType.DMA
-    new_keys, new_values, new_counts, attended = pl.pallas_call(
+    shapes = (
+        jax.ShapeDtypeStruct((owned, width), F32),
+        jax.ShapeDtypeStruct((owned, width), F32),
+        jax.ShapeDtypeStruct((1, owned), F32),
+        jax.ShapeDtypeStruct((share, width), BF16),
+    )
+    results = pl.pallas_call(
         functools.partial(kernel, nctx, nhead, owned, steps, width),
-        out_shape=(
-            jax.ShapeDtypeStruct((owned, width), F32),
-            jax.ShapeDtypeStruct((owned, width), F32),
-            jax.ShapeDtypeStruct((1, owned), F32),
-            jax.ShapeDtypeStruct((share, width), BF16),
-        ),
+        out_shape=shapes,
         in_specs=[hbm] * 11,
         out_specs=(vmem,) * 4,
         scratch_shapes=[
@@ -463,21 +459,17 @@
             pltpu.VMEM((rows, 128), F32),
             pltpu.VMEM((2, tokens // 128, 128), F32),
             pltpu.VMEM((nz, owned, 2 * width), F32),
-            pltpu.VMEM((nz, owned, 2 * width), BF16),
-            pltpu.VMEM((nz, owned, 2 * width), BF16),
-            pltpu.VMEM((16, owned, width), BF16),
-            pltpu.VMEM((16, owned, width), BF16),
+            pltpu.VMEM((nz, owned + 16, 2 * width), BF16),
+            pltpu.VMEM((nz, owned + 16, 2 * width), BF16),
+            pltpu.VMEM((16, owned + 16, width), BF16),
+            pltpu.VMEM((16, owned + 16, width), BF16),
             pltpu.VMEM((nhead, rows // nhead, width), BF16),
             pltpu.VMEM((nhead, rows // nhead, width), BF16),
             pltpu.VMEM((nctx, 8, 128), F32),
-            pltpu.VMEM((nctx, 8, 128), F32),
-            pltpu.VMEM((nctx, share, width), BF16),
-            pltpu.VMEM((nctx, share, width), BF16),
-            pltpu.VMEM((nctx, 1, 128), F32),
-            pltpu.VMEM((nctx, 1, 128), F32),
+            pltpu.VMEM((nctx, 2 * share, width), BF16),
+            pltpu.VMEM((nctx, 2 * share, width), BF16),
             dma((11,)),
-            dma((nhead,)), dma((nhead,)), dma((nctx,)), dma((nctx,)), dma((nz,)), dma((nz,)),
-            dma((16,)), dma((16,)), dma((nctx,)), dma((nctx,)), dma((nctx,)), dma((nctx,)),
+            dma(()), dma(()), dma((nz,)), dma((nz,)), dma((16,)), dma((16,)), dma(()), dma(()),
         ],
         compiler_params=pltpu.CompilerParams(
             collective_id=0, has_side_effects=True, vmem_limit_bytes=60000000
@@ -491,6 +483,13 @@
         queries.reshape(rows, width),
         stretch_keys, stretch_values, cache_keys, cache_values, centroid_keys, centroid_values,
     )
+    new_keys, new_values, new_counts, attended = pl.pallas_call(
+        finish_kernel,
+        out_shape=shapes,
+        in_specs=[vmem] * 4,
+        out_specs=(vmem,) * 4,
+        name="finish",
+    )(*results)
     return (
         new_keys[None],
         new_values[None],

time: 50.8 us -> 45.9 us (0.904)
  local copies, waits for them, and re-layouts: 5.64 us -> 0 us
  Pallas kernels: 44.3 us -> 45.1 us
    unnamed x4 -> x0, local copies, waits for them, and re-layouts: 5.64 us -> none
    pallas_call x0 -> x1, Pallas kernels: none -> 1.69 us  [shards(): pl.pallas_call(finish_kernel, out_shape=shapes, in_specs=[vmem] * 4, out_...]
    pallas_call x1, Pallas kernels: 44.3 us -> 43.4 us  [shards(): pl.pallas_call(functools.partial(kernel, nctx, nhead, owned, steps, width...]
where the time goes in v3:
time: 45.9 us; the launch traced here: 45.8 us
  Pallas kernels  45.1 us (98%)
  between operations  0.64 us (1%)
    pallas_call x1, Pallas kernels, shards(): pl.pallas_call(functools.partial(kernel, nctx, nhead, owned, steps, width...  43.4 us
    pallas_call x1, Pallas kernels, shards(): pl.pallas_call(finish_kernel, out_shape=shapes, in_specs=[vmem] * 4, out_...  1.69 us

profile of v3, /device:TPU:1, one launch (start us, length us, event | category | flops | bytes accessed | tf_op | source)
XLA Modules:
  0.0 45.8 jit_solution(2897663793910720915)
XLA Ops:
  0.6 43.4 %retrieve.1 = (f32[256,128]{1,0:T(8,128)}, f32[256,128]{1,0:T(8,128)}, f32[1,256]{1,0:T(1,128)}, bf16[16,128]{1,0:T(8,128)(2,1)}) custom-call(s32[4,64]{1,0:T(4,128)} %bitcast.12, s32[32,128]{1,0:T(8,128)} %bitcast.10, s32[1,512]{1,0:T(1,128)} %blocks_in.1, f32[32,128]{1,0:T(8,128)} %bitcast.11, bf16[256,128]{1,0:T(8,128)(2,1)} %bitcast.9, ...), custom_call_target="tpu_custom_call" | custom-call | tf_op jit(solution)/shard_map/retrieve/pallas_call | solution.py:441
  44.1 1.7 %finish.1 = (f32[256,128]{1,0:T(8,128)}, f32[256,128]{1,0:T(8,128)}, f32[1,256]{1,0:T(1,128)}, bf16[16,128]{1,0:T(8,128)(2,1)}) custom-call(f32[256,128]{1,0:T(8,128)} %get-tuple-element.12.k_in, f32[256,128]{1,0:T(8,128)} %get-tuple-element.13.v_in, f32[1,256]{1,0:T(1,128)} %get-tuple-element.14.n_in, bf16[16,128]{1,0:T(8,128)(2,1)} %get-tuple-element.15.a_in), custom_call_target="tpu_custom_call" | custom-call | tf_op jit(solution)/shard_map/finish/pallas_call | solution.py:486

commit v4 on v3

--- a/solution.py
+++ b/solution.py
@@ -34,7 +34,7 @@
     nctx, nhead, owned, steps, width,
     sel_in, assign_in, blocks_in, counts_in, queries_in, skeys, svals, ckeys, cvals, cent_k, cent_v,
     out_k, out_v, out_n, out_a,
-    sel, assign, blocks, old_counts, queries, kv, cen, hits, bias, scores, mrun, acc, lrun, rel, own,
+    sel, assign, blocks, old_counts, queries, kv, cen, member, bias, scores, mrun, acc, lrun, rel, own,
     sib_send, sib_recv, ring_send, ring_recv, qsend, qrecv, named, fsend, frecv,
     load_sem, q_ss, q_rs, s_ss, s_rs, r_ss, r_rs, f_ss, f_rs,
 ):
@@ -204,9 +204,9 @@
         lax.fori_loop(1, count, step, 0)
 
     used = owned // 128
-    r = lax.broadcasted_iota(jnp.int32, (nctx * 8, 128), 0)
-    pattern = jnp.where(lax.rem(r, 8) < used, (r // 8) * used + lax.rem(r, 8), -1)
-    pattern = pattern.astype(F32).astype(BF16).reshape(nctx * 8 // 16, 16, 128)
+    high_rows = nctx * used
+    pattern = lax.broadcasted_iota(jnp.int32, (high_rows, 128), 0).astype(F32).astype(BF16)
+    pattern = pattern.reshape(high_rows // 16, 16, 128)
     lanes = lax.broadcasted_iota(jnp.int32, (128, 128), 0).astype(F32).astype(BF16).reshape(8, 16, 128)
     rel[0] = lax.shift_right_logical(ids, 7).astype(F32)
     rel[1] = (ids & 127).astype(F32)
@@ -219,7 +219,9 @@
             pieces.append(jnp.where(equal, jnp.ones((), BF16), jnp.zeros((), BF16)).reshape(-1, 128))
         both.append(jnp.concatenate(pieces, axis=1))
     tally = lax.dot_general(both[0], both[1], NT, preferred_element_type=F32)
-    named[...] = tally.reshape(nctx, 8, 128)
+    named[...] = jnp.zeros_like(named)
+    for k in range(nctx):
+        named[k, 0:used, :] = tally[k * used : (k + 1) * used]
 
     r_out = lax.broadcasted_iota(jnp.int32, (rows, rows), 0)
     r_in = lax.broadcasted_iota(jnp.int32, (rows, rows), 1)
@@ -237,10 +239,22 @@
     start_ring()
     segment(2, 5)
 
-    nblk = blocks.shape[1]
     small[2].wait()
     small[3].wait()
     small[4].wait()
+    picks = sel.shape[1]
+    hi_rows = lax.broadcasted_iota(jnp.int32, (high_rows, picks), 0)
+    lo_rows = lax.broadcasted_iota(jnp.int32, (128, picks), 0)
+    bits = jnp.zeros((high_rows, 128), jnp.int32)
+    for s in range(steps):
+        chosen = sel[s : s + 1, :]
+        hi_hot = (hi_rows == lax.shift_right_logical(chosen, 7)).astype(F32).astype(BF16)
+        lo_hot = (lo_rows == (chosen & 127)).astype(F32).astype(BF16)
+        found = lax.dot_general(hi_hot, lo_hot, NT, preferred_element_type=F32)
+        bits = bits + jnp.where(found > 0.5, 1 << s, 0)
+    member[...] = bits
+
+    nblk = blocks.shape[1]
     lane = lax.broadcasted_iota(jnp.int32, (16, 128), 1)
     sub = lax.broadcasted_iota(jnp.int32, (16, 128), 0)
     spread = sub * 8 + lane // 16
@@ -248,31 +262,18 @@
     for q in range(nblk // 128):
         source = jnp.broadcast_to(blocks[:, q * 128 : (q + 1) * 128], (16, 128))
         expanded.append(jnp.take_along_axis(source, spread, axis=1, mode="promise_in_bounds"))
-    mine = me * owned + lax.broadcasted_iota(jnp.int32, (8, 128), 0) * 128
-    mine = mine + lax.broadcasted_iota(jnp.int32, (8, 128), 1)
-    dense = jnp.concatenate([ids] + expanded + [mine], axis=0)
-    trows, crows = tokens // 128, cached // 128
-    for s in range(steps):
-
-        def hit(i, seen):
-            return seen | (dense == sel[s, i]).astype(jnp.int32)
-
-        seen = lax.fori_loop(0, sel.shape[1], hit, jnp.zeros(dense.shape, jnp.int32), unroll=8)
-        hits[s, 0 : trows + crows, :] = jnp.where(seen[: trows + crows] > 0, 0.0, MASKED)
-        hits[s, trows + crows :, :] = jnp.where(seen[trows + crows :] > 0, MASKED, 0.0)
-
+    dense = jnp.concatenate([ids] + expanded, axis=0)
+    hi, lo = lax.shift_right_logical(dense, 7), dense & 127
+    seen = jnp.zeros(dense.shape, jnp.int32)
+    for r in range(high_rows):
+        row = jnp.broadcast_to(bits[r : r + 1, :], dense.shape)
+        seen = jnp.where(hi == r, jnp.take_along_axis(row, lo, axis=1, mode="promise_in_bounds"), seen)
     wide = TILE // 128
-    copies = share // steps
-
-    def spread_bias(n, _):
+    mask_of = lax.shift_left(jnp.ones((share, 128), jnp.int32), sub // (share // steps))
+    for n in range(tiles):
         for u in range(wide):
-            per_step = [
-                jnp.broadcast_to(hits[s, pl.ds(n * wide + u, 1), :], (copies, 128)) for s in range(steps)
-            ]
-            bias[n, :, u * 128 : (u + 1) * 128] = jnp.concatenate(per_step, axis=0)
-        return 0
-
-    lax.fori_loop(0, tiles, spread_bias, 0)
+            picked = jnp.broadcast_to(seen[n * wide + u : n * wide + u + 1, :], (share, 128)) & mask_of
+            bias[n, :, u * 128 : (u + 1) * 128] = jnp.where(picked != 0, 0.0, MASKED)
 
     forward(1, 3, 0, 1)
     forward(2, 5, 1, 1)
@@ -350,12 +351,10 @@
         out_n[:, u * 128 : (u + 1) * 128] = after[u : u + 1, :]
     log_counts = jnp.log(after) * LOG2E
     centre_bias = []
+    own_bits = member[pl.ds(me * used, used), :]
     for u in range(used):
-        per_step = [
-            jnp.broadcast_to(hits[s, trows + crows + u : trows + crows + u + 1, :], (copies, 128))
-            for s in range(steps)
-        ]
-        centre_bias.append(jnp.concatenate(per_step, axis=0) + log_counts[u : u + 1, :])
+        picked = jnp.broadcast_to(own_bits[u : u + 1, :], (share, 128)) & mask_of
+        centre_bias.append(jnp.where(picked != 0, MASKED, 0.0) + log_counts[u : u + 1, :])
     centre_bias = jnp.concatenate(centre_bias, axis=1)
 
     new = []
@@ -387,7 +386,11 @@
     high, mid, low = (x.astype(F32) for x in split3(lse))
     three = jnp.where(spot == 0, high, jnp.where(spot == 1, mid, jnp.where(spot == 2, low, 0.0)))
     fsend[:, share:, :] = three.astype(BF16).reshape(nctx, share, 128)
-    each(nctx, lambda k: row_copy(k).start())
+    half = nctx // 2
+    row_copy(half).start()
+    for k in range(1, half):
+        row_copy(half - k).start()
+        row_copy(half + k).start()
     frecv[me] = fsend[me]
     for copy in hops:
         copy.wait_send()
@@ -444,14 +447,14 @@
         in_specs=[hbm] * 11,
         out_specs=(vmem,) * 4,
         scratch_shapes=[
-            pltpu.SMEM((steps, selected.shape[2]), jnp.int32),
+            pltpu.VMEM((steps, selected.shape[2]), jnp.int32),
             pltpu.VMEM((tokens // 128, 128), jnp.int32),
             pltpu.VMEM(block_cluster.shape, jnp.int32),
             pltpu.VMEM((clusters // 128, 128), F32),
             pltpu.VMEM((rows, width), BF16),
             pltpu.VMEM((tokens + cached, 2 * width), BF16),
             pltpu.VMEM((2, owned, width), F32),
-            pltpu.VMEM((steps, (tokens + cached) // 128 + 8, 128), F32),
+            pltpu.VMEM((clusters // 128, 128), jnp.int32),
             pltpu.VMEM((tiles, share, TILE), F32),
             pltpu.VMEM((tiles, rows, TILE), F32),
             pltpu.VMEM((rows, 128), F32),

time: 45.9 us -> 44.7 us (0.974)
  Pallas kernels: 45.1 us -> 43.8 us
    pallas_call x1, Pallas kernels: 43.4 us -> 42.2 us  [shards(): pl.pallas_call(functools.partial(kernel, nctx, nhead, owned, steps, width...]
where the time goes in v4:
time: 44.7 us; the launch traced here: 44.5 us
  Pallas kernels  43.8 us (98%)
  between operations  0.64 us (1%)
    pallas_call x1, Pallas kernels, shards(): pl.pallas_call(functools.partial(kernel, nctx, nhead, owned, steps, width...  42.2 us
    pallas_call x1, Pallas kernels, shards(): pl.pallas_call(finish_kernel, out_shape=shapes, in_specs=[vmem] * 4, out_...  1.69 us

profile of v4, /device:TPU:1, one launch (start us, length us, event | category | flops | bytes accessed | tf_op | source)
XLA Modules:
  0.0 44.5 jit_solution(135124326353033880)
XLA Ops:
  0.6 42.2 %retrieve.1 = (f32[256,128]{1,0:T(8,128)}, f32[256,128]{1,0:T(8,128)}, f32[1,256]{1,0:T(1,128)}, bf16[16,128]{1,0:T(8,128)(2,1)}) custom-call(s32[4,64]{1,0:T(4,128)} %bitcast.12, s32[32,128]{1,0:T(8,128)} %bitcast.10, s32[1,512]{1,0:T(1,128)} %blocks_in.1, f32[32,128]{1,0:T(8,128)} %bitcast.11, bf16[256,128]{1,0:T(8,128)(2,1)} %bitcast.9, ...), custom_call_target="tpu_custom_call" | custom-call | tf_op jit(solution)/shard_map/retrieve/pallas_call | solution.py:444
  42.8 1.7 %finish.1 = (f32[256,128]{1,0:T(8,128)}, f32[256,128]{1,0:T(8,128)}, f32[1,256]{1,0:T(1,128)}, bf16[16,128]{1,0:T(8,128)(2,1)}) custom-call(f32[256,128]{1,0:T(8,128)} %get-tuple-element.12.k_in, f32[256,128]{1,0:T(8,128)} %get-tuple-element.13.v_in, f32[1,256]{1,0:T(1,128)} %get-tuple-element.14.n_in, bf16[16,128]{1,0:T(8,128)(2,1)} %get-tuple-element.15.a_in), custom_call_target="tpu_custom_call" | custom-call | tf_op jit(solution)/shard_map/finish/pallas_call | solution.py:489

commit v5 on v4

--- a/solution.py
+++ b/solution.py
@@ -14,7 +14,7 @@
 LOG2E = math.log2(math.e)
 MASKED = -1e30
 FLOOR = -1e29
-TILE = 2048
+TILE = 3072
 NT = (((1,), (1,)), ((), ()))
 
 
@@ -113,9 +113,6 @@
         sib_send[j, owned:, 0:width] = counts_out(named[2 * zd + 1 - core])
         sib_send[j, owned:, width:] = jnp.zeros((16, width), BF16)
         own[j] = sums[owned : 2 * owned]
-        if j == 0:
-            pl.semaphore_wait(barrier, nctx - 1 + nhead - 1)
-        sibling(j).start()
 
     def sibling(j):
         return pltpu.make_async_remote_copy(
@@ -230,15 +227,6 @@
     small[1].wait()
     qsend[...] = jnp.dot(order, queries[...], preferred_element_type=F32).astype(BF16).reshape(nhead, per, width)
 
-    loads[0].wait()
-    loads[1].wait()
-    segment(0, 4)
-    each(nhead, lambda k: query_copy(k).start())
-    qrecv[head] = qsend[head]
-    segment(1, 3)
-    start_ring()
-    segment(2, 5)
-
     small[2].wait()
     small[3].wait()
     small[4].wait()
@@ -253,6 +241,10 @@
         found = lax.dot_general(hi_hot, lo_hot, NT, preferred_element_type=F32)
         bits = bits + jnp.where(found > 0.5, 1 << s, 0)
     member[...] = bits
+
+    loads[0].wait()
+    loads[1].wait()
+    segment(0, 4)
 
     nblk = blocks.shape[1]
     lane = lax.broadcasted_iota(jnp.int32, (16, 128), 1)
@@ -275,11 +267,21 @@
             picked = jnp.broadcast_to(seen[n * wide + u : n * wide + u + 1, :], (share, 128)) & mask_of
             bias[n, :, u * 128 : (u + 1) * 128] = jnp.where(picked != 0, 0.0, MASKED)
 
+    pl.semaphore_wait(barrier, nctx - 1 + nhead - 1)
+    sibling(0).start()
+    each(nhead, lambda k: query_copy(k).start())
+    qrecv[head] = qsend[head]
+    segment(1, 3)
+    segment(2, 5)
+    sibling(1).start()
+    sibling(2).start()
+    start_ring()
+    segment(3, 2)
+    segment(4, 6)
+    sibling(3).start()
+    sibling(4).start()
     forward(1, 3, 0, 1)
     forward(2, 5, 1, 1)
-
-    segment(3, 2)
-    segment(4, 6)
 
     all_queries().wait_recv()
     q = qrecv[...].reshape(rows, width)
@@ -301,14 +303,17 @@
     loads[3].wait()
     lax.fori_loop(0, tiles // 2, score, 0)
 
+    segment(5, 1)
+    segment(6, 7)
+    sibling(5).start()
+    sibling(6).start()
     forward(3, 2, 0, 2)
     forward(4, 6, 1, 2)
-    segment(5, 1)
-    segment(6, 7)
     lax.fori_loop(tiles // 2, tiles, score, 0)
+    segment(7, 0)
+    sibling(7).start()
     forward(5, 1, 0, 3)
     forward(6, 7, 1, 3)
-    segment(7, 0)
 
     top_here = jnp.max(mrun[...], axis=1, keepdims=True)
     mrun[...] = jnp.broadcast_to(top_here, mrun.shape)

time: 44.7 us -> 41.4 us (0.926)
  Pallas kernels: 43.8 us -> 40.6 us
    pallas_call x1, Pallas kernels: 42.2 us -> 38.9 us  [shards(): pl.pallas_call(functools.partial(kernel, nctx, nhead, owned, steps, width...]
where the time goes in v5:
time: 41.4 us; the launch traced here: 41.2 us
  Pallas kernels  40.6 us (98%)
  between operations  0.64 us (2%)
    pallas_call x1, Pallas kernels, shards(): pl.pallas_call(functools.partial(kernel, nctx, nhead, owned, steps, width...  38.9 us
    pallas_call x1, Pallas kernels, shards(): pl.pallas_call(finish_kernel, out_shape=shapes, in_specs=[vmem] * 4, out_...  1.69 us

profile of v5, /device:TPU:1, one launch (start us, length us, event | category | flops | bytes accessed | tf_op | source)
XLA Modules:
  0.0 41.2 jit_solution(9346803893401035053)
XLA Ops:
  0.6 38.9 %retrieve.1 = (f32[256,128]{1,0:T(8,128)}, f32[256,128]{1,0:T(8,128)}, f32[1,256]{1,0:T(1,128)}, bf16[16,128]{1,0:T(8,128)(2,1)}) custom-call(s32[4,64]{1,0:T(4,128)} %bitcast.12, s32[32,128]{1,0:T(8,128)} %bitcast.10, s32[1,512]{1,0:T(1,128)} %blocks_in.1, f32[32,128]{1,0:T(8,128)} %bitcast.11, bf16[256,128]{1,0:T(8,128)(2,1)} %bitcast.9, ...), custom_call_target="tpu_custom_call" | custom-call | tf_op jit(solution)/shard_map/retrieve/pallas_call | solution.py:449
  39.5 1.7 %finish.1 = (f32[256,128]{1,0:T(8,128)}, f32[256,128]{1,0:T(8,128)}, f32[1,256]{1,0:T(1,128)}, bf16[16,128]{1,0:T(8,128)(2,1)}) custom-call(f32[256,128]{1,0:T(8,128)} %get-tuple-element.12.k_in, f32[256,128]{1,0:T(8,128)} %get-tuple-element.13.v_in, f32[1,256]{1,0:T(1,128)} %get-tuple-element.14.n_in, bf16[16,128]{1,0:T(8,128)(2,1)} %get-tuple-element.15.a_in), custom_call_target="tpu_custom_call" | custom-call | tf_op jit(solution)/shard_map/finish/pallas_call | solution.py:494

commit v6 on v5

--- a/solution.py
+++ b/solution.py
@@ -136,7 +136,6 @@
         if half == 0:
             count = named[2 * lax.rem(z + offset, nz) + core] + counts_in(sib_recv[j, owned:, 0:width])
         for direction, step in arrivals:
-            hop(direction, step, half).wait_recv()
             at = (direction * 4 + step) * 2 + half
             value = value + ring_recv[at, 0:owned, :].astype(F32)
             if half == 0:
@@ -145,29 +144,28 @@
 
     hops = []
 
-    def launch(j, offset, direction, step, half, arrivals):
-        at = (direction * 4 + step) * 2 + half
-        value, count = mixed(j, offset, half, arrivals)
-        ring_send[at, 0:owned, :] = value.astype(BF16)
-        if half == 0:
-            ring_send[at, owned:, :] = counts_out(count)
-        copy = hop(direction, step, half)
-        copy.start()
-        hops.append(copy)
-
-    def forward(j, offset, direction, step):
-        sibling(j).wait_recv()
-        first = 0 if direction == 0 else 1
-        for half in (first, 1 - first):
-            arrivals = []
-            if step >= 2 or (step == 1 and half == first):
-                arrivals = [(direction, step - 1)]
-            launch(j, offset, direction, step, half, arrivals)
-
-    def start_ring():
-        sibling(0).wait_recv()
-        for direction in (0, 1):
-            launch(0, 4, direction, 0, direction, [])
+    def forward(*moves):
+        plans = []
+        for j, offset, direction, step in moves:
+            first = direction
+            for half in (first, 1 - first) if step > 0 else (first,):
+                arrivals = [(direction, step - 1)] if step >= 2 or (step == 1 and half == first) else []
+                plans.append((j, offset, direction, step, half, arrivals))
+        for j in sorted({move[0] for move in moves}):
+            sibling(j).wait_recv()
+        for _, _, _, _, half, arrivals in plans:
+            for direction, step in arrivals:
+                hop(direction, step, half).wait_recv()
+        for j, offset, direction, step, half, arrivals in plans:
+            at = (direction * 4 + step) * 2 + half
+            value, count = mixed(j, offset, half, arrivals)
+            ring_send[at, 0:owned, :] = value.astype(BF16)
+            if half == 0:
+                ring_send[at, owned:, :] = counts_out(count)
+        for _, _, direction, step, half, _ in plans:
+            copy = hop(direction, step, half)
+            copy.start()
+            hops.append(copy)
 
     def query_copy(k):
         to = lax.rem(head + k, nhead)
@@ -269,19 +267,18 @@
 
     pl.semaphore_wait(barrier, nctx - 1 + nhead - 1)
     sibling(0).start()
-    each(nhead, lambda k: query_copy(k).start())
-    qrecv[head] = qsend[head]
     segment(1, 3)
     segment(2, 5)
     sibling(1).start()
     sibling(2).start()
-    start_ring()
+    forward((0, 4, 0, 0), (0, 4, 1, 0))
+    each(nhead, lambda k: query_copy(k).start())
+    qrecv[head] = qsend[head]
     segment(3, 2)
     segment(4, 6)
     sibling(3).start()
     sibling(4).start()
-    forward(1, 3, 0, 1)
-    forward(2, 5, 1, 1)
+    forward((1, 3, 0, 1), (2, 5, 1, 1))
 
     all_queries().wait_recv()
     q = qrecv[...].reshape(rows, width)
@@ -307,13 +304,11 @@
     segment(6, 7)
     sibling(5).start()
     sibling(6).start()
-    forward(3, 2, 0, 2)
-    forward(4, 6, 1, 2)
+    forward((3, 2, 0, 2), (4, 6, 1, 2))
     lax.fori_loop(tiles // 2, tiles, score, 0)
     segment(7, 0)
     sibling(7).start()
-    forward(5, 1, 0, 3)
-    forward(6, 7, 1, 3)
+    forward((5, 1, 0, 3), (6, 7, 1, 3))
 
     top_here = jnp.max(mrun[...], axis=1, keepdims=True)
     mrun[...] = jnp.broadcast_to(top_here, mrun.shape)
@@ -339,6 +334,9 @@
     loads[5].wait()
     sibling(7).wait_recv()
     ends = [(0, 3), (1, 3)]
+    for direction, step in ends:
+        for half in (0, 1):
+            hop(direction, step, half).wait_recv()
     key_sums, added = mixed(7, 0, 0, ends)
     value_sums, _ = mixed(7, 0, 1, ends)
     added = added[0:used]

time: 41.4 us -> 41.2 us (level)
  no operation moved by 1% of the time
where the time goes in v6:
time: 41.2 us; the launch traced here: 41 us
  Pallas kernels  40.4 us (98%)
  between operations  0.64 us (2%)
    pallas_call x1, Pallas kernels, shards(): pl.pallas_call(functools.partial(kernel, nctx, nhead, owned, steps, width...  38.7 us
    pallas_call x1, Pallas kernels, shards(): pl.pallas_call(finish_kernel, out_shape=shapes, in_specs=[vmem] * 4, out_...  1.69 us

profile of v6, /device:TPU:1, one launch (start us, length us, event | category | flops | bytes accessed | tf_op | source)
XLA Modules:
  0.0 41.0 jit_solution(1225853658934700318)
XLA Ops:
  0.6 38.7 %retrieve.1 = (f32[256,128]{1,0:T(8,128)}, f32[256,128]{1,0:T(8,128)}, f32[1,256]{1,0:T(1,128)}, bf16[16,128]{1,0:T(8,128)(2,1)}) custom-call(s32[4,64]{1,0:T(4,128)} %bitcast.12, s32[32,128]{1,0:T(8,128)} %bitcast.10, s32[1,512]{1,0:T(1,128)} %blocks_in.1, f32[32,128]{1,0:T(8,128)} %bitcast.11, bf16[256,128]{1,0:T(8,128)(2,1)} %bitcast.9, ...), custom_call_target="tpu_custom_call" | custom-call | tf_op jit(solution)/shard_map/retrieve/pallas_call | solution.py:447
  39.3 1.7 %finish.1 = (f32[256,128]{1,0:T(8,128)}, f32[256,128]{1,0:T(8,128)}, f32[1,256]{1,0:T(1,128)}, bf16[16,128]{1,0:T(8,128)(2,1)}) custom-call(f32[256,128]{1,0:T(8,128)} %get-tuple-element.12.k_in, f32[256,128]{1,0:T(8,128)} %get-tuple-element.13.v_in, f32[1,256]{1,0:T(1,128)} %get-tuple-element.14.n_in, bf16[16,128]{1,0:T(8,128)(2,1)} %get-tuple-element.15.a_in), custom_call_target="tpu_custom_call" | custom-call | tf_op jit(solution)/shard_map/finish/pallas_call | solution.py:492
